TPU v7x, 512 devices: a whole 4x8x8 slice. The times are simulated.
512 devices in a mesh: tm: 8 (over x, y_lo), space: 64 (over z, y_hi, core).
Axes of the slice: x: 4, y: 8 (y_hi: 4, y_lo: 2; y = y_hi * 2 + y_lo), z: 8, core: 2. Of those that a mesh axis runs over, the one named last changes fastest.
Arguments:
- lam: float32 [8, 72, 512, 256], P('tm', None, 'space'), may hold values from -6 to 6
- obs_mult: float32 [8, 16384], P('tm', 'space'), may hold values from -6 to 6
- dx: float32 [8, 72, 512, 256], P('tm', None, 'space'), may hold values from -6 to 6
- fresh_state: float32 [2, 72, 512, 256], P(None, None, 'space'), may hold values from -6 to 6
- fresh_obs: float32 [16384], P('space'), may hold values from -6 to 6
- sigma: float32 [8, 72], P('tm'), may hold values from 0.3 to 3
- obs_var: float32 [16384], P('space'), may hold values from 0.5 to 2
- obs_idx: int32 [16384], P('space'), may hold values from 0 to 147455
- stencil_coef: float32 [3, 512, 256], P(None, 'space'), may hold values from 0.05 to 0.25
- vert_cov: float32 [72, 72], replicated, may hold values from -0.75 to 0.75
- block_pattern: int32 [9, 9], replicated, may hold values 0 or 1
Outputs:
- out_lam: float32 [8, 72, 512, 256], P('tm', None, 'space')
- out_obs: float32 [8, 16384], P('tm', 'space')
- out_dx: float32 [8, 72, 512, 256], P('tm', None, 'space')
Inputs may be any that keep to these rules, and one draw needn't show every extreme that they name: `obs_idx`: a row-major index (level, row, column) into the observation's tile of 72 x 8 x 256 cells.
All inputs are finite; a program needn't handle non-finite values.
Results may differ from a plain program's by a relative error of at most 0.00007.
Values sent between devices are 32-bit elements; how exact they have to be, the bound alone decides.
A program may use at most 64 MiB of HBM per device.

v0:
```python
import jax
import jax.numpy as jnp
from jax import lax
from jax.sharding import PartitionSpec as P

LB = 8
STEPS = 2


def extended(block, sides, width):
    for axis, dim in sides:
        count = lax.axis_size(axis)
        forward = [(i, i + 1) for i in range(count - 1)]
        backward = [(target, source) for source, target in forward]
        low = lax.ppermute(
            lax.slice_in_dim(block, block.shape[dim] - width, None, axis=dim), axis, forward
        )
        high = lax.ppermute(lax.slice_in_dim(block, 0, width, axis=dim), axis, backward)
        block = jnp.concatenate([low, block, high], axis=dim)
    return block


def passed_along(block, axis, distance):
    devices = range(lax.axis_size(axis))
    route = [(i - distance, i) for i in devices if i - distance in devices]
    return lax.ppermute(block, axis, route)


def tl_advance(ext, coef):
    center = ext[:, :, 2:-2]
    return (
        center
        + coef[0] * (ext[:, :, 3:-1] + ext[:, :, 1:-3] - 2.0 * center)
        + coef[1] * (ext[:, :, 4:] + ext[:, :, :-4] - 2.0 * center)
        + coef[2] * (jnp.roll(center, 1, axis=3) - center)
    )


def adj_advance(ext, coef):
    center = ext[:, :, 2:-2]
    near = coef[0] * ext
    far_rows = coef[1] * ext
    cols = coef[2, 2:-2] * center
    result = (
        center
        + (near[:, :, 3:-1] + near[:, :, 1:-3] - 2.0 * near[:, :, 2:-2])
        + (far_rows[:, :, 4:] + far_rows[:, :, :-4] - 2.0 * far_rows[:, :, 2:-2])
        + (jnp.roll(cols, -1, axis=3) - cols)
    )
    return result * coef[3, 2:-2]


def forward_model(field, coef_ext):
    rows = field.shape[2]
    depth = 2 * STEPS
    current = field
    for step in range(STEPS):
        ext = extended(current, (("space", 2),), 2)
        current = tl_advance(ext, coef_ext[:, depth : depth + rows])
    return current


def adjoint_model(field, coef_ext):
    rows = field.shape[2]
    depth = 2 * STEPS
    current = field
    first_ext = None
    width = 2
    for step in range(STEPS):
        ext = extended(current, (("space", 2),), 2)
        if step == 0:
            first_ext = ext
        current = adj_advance(ext, coef_ext[:, depth - 2 : depth + rows + 2])
    return (current, first_ext, width)


def covariance(lam, sigma, vertical):
    scale = sigma[:, :, None, None]
    scaled = scale * lam
    ext = extended(scaled, (("space", 2),), 1)
    smooth = scaled + 0.1 * (
        ext[:, :, 2:]
        + ext[:, :, :-2]
        - 2.0 * scaled
        + (jnp.roll(scaled, 1, axis=3) + jnp.roll(scaled, -1, axis=3) - 2.0 * scaled)
    )
    return scale * jnp.einsum("lm,smyx->slyx", vertical, smooth, precision=lax.Precision.HIGHEST)


def saddle(lam, mult, dx, tl_term, sigma, obs_var, obs_idx, coef_ext, vertical):
    count = dx.shape[0]
    back, lam_ext, width = adjoint_model(lam, coef_ext)
    arrived = passed_along(back[0], "tm", -1)
    ad_term = jnp.concatenate([back[1:], arrived[None]], axis=0)
    p_lam = covariance(lam, sigma, vertical) + (dx - tl_term)
    flat = dx.reshape(count, -1)
    p_mu = obs_var[None, :] * mult + jnp.take(flat, obs_idx, axis=1)
    spread = jnp.zeros_like(flat).at[:, obs_idx].add(mult).reshape(dx.shape)
    p_dx = lam - ad_term + spread
    return (p_lam, p_mu, p_dx)


def local(
    lam,
    obs_mult,
    dx,
    fresh_state,
    fresh_obs,
    sigma,
    obs_var,
    obs_idx,
    stencil_coef,
    vert_cov,
    block_pattern,
):
    levels = dx.shape[1]
    blocks_n = block_pattern.shape[0]
    ones_row = jnp.ones((1,) + stencil_coef.shape[1:], jnp.float32)
    coef_all = jnp.concatenate([stencil_coef, ones_row], axis=0)
    coef_ext = extended(coef_all, (("space", 1),), 2 * STEPS)
    blocks = jnp.maximum(block_pattern, jnp.eye(blocks_n, dtype=jnp.int32))
    keep = jnp.repeat(jnp.repeat(blocks, LB, axis=0), LB, axis=1).astype(jnp.float32)
    vertical = 2.0 * jnp.eye(levels, dtype=jnp.float32) + keep * vert_cov
    moved = forward_model(dx, coef_ext)
    incoming = passed_along(moved[-1], "tm", 1)
    tl_term = jnp.concatenate([incoming[None], moved[:-1]], axis=0)
    p_lam, p_mu, p_dx = saddle(
        lam, obs_mult, dx, tl_term, sigma, obs_var, obs_idx, coef_ext, vertical
    )
    leading = jnp.stack([p_lam[0], p_dx[0]])
    got_state, got_obs = passed_along((leading, p_mu[0]), "tm", -1)
    is_last = lax.axis_index("tm") == lax.axis_size("tm") - 1
    got_state = jnp.where(is_last, fresh_state, got_state)
    got_obs = jnp.where(is_last, fresh_obs, got_obs)
    lam_two = jnp.concatenate([p_lam[1:], got_state[0][None]], axis=0)
    dx_two = jnp.concatenate([p_dx[1:], got_state[1][None]], axis=0)
    mu_two = jnp.concatenate([p_mu[1:], got_obs[None]], axis=0)
    advanced = forward_model(dx_two, coef_ext)
    handed = passed_along(advanced[-1], "tm", 1)
    tl_two = jnp.concatenate([handed[None], advanced[:-1]], axis=0)
    out_lam, out_obs, out_dx = saddle(
        lam_two, mu_two, dx_two, tl_two, sigma, obs_var, obs_idx, coef_ext, vertical
    )
    return (out_lam, out_obs, out_dx)


def solution(mesh):
    in_specs = (
        P("tm", None, "space", None),
        P("tm", "space"),
        P("tm", None, "space", None),
        P(None, None, "space", None),
        P("space"),
        P("tm", None),
        P("space"),
        P("space"),
        P(None, "space", None),
        P(),
        P(),
    )
    out_specs = (P("tm", None, "space", None), P("tm", "space"), P("tm", None, "space", None))
    return jax.shard_map(local, mesh=mesh, in_specs=in_specs, out_specs=out_specs, check_vma=False)
```

profile of v0, /device:TPU:253, one launch (start us, length us, event | category | flops | bytes accessed | tf_op | source)
XLA Modules:
  0.0 233.9 jit_solution(14158594458057089071)
XLA Ops:
  0.7 1.5 fusion.159
  2.2 6.0 %collective-permute-start.3 = (f32[1,72,2,256]{3,1,2,0:T(8,128)S(1)}, f32[1,72,2,256]{3,1,2,0:T(8,128)S(1)}, u32[]{:S(2)}, u32[]{:S(2)}) collective-permute-start(f32[1,72,2,256]{3,1,2,0:T(8,128)S(1)} %copy.109), channel_id=1, source_target_pairs={{0,1},{1,2},{2,3},{3,4},{4,5},{5,6},{6,7},{7,8},{8,9},{9,10},{10,1... | collective-permute-start | bytes 442376 | tf_op jit(solution)/shard_map/ppermute | solution.py:15
  8.2 1.9 collective-permute-start.2
  10.2 7.9 %collective-permute-start.9 = (f32[1,72,2,256]{3,1,2,0:T(8,128)S(1)}, f32[1,72,2,256]{3,1,2,0:T(8,128)S(1)}, u32[]{:S(2)}, u32[]{:S(2)}) collective-permute-start(f32[1,72,2,256]{3,1,2,0:T(8,128)S(1)} %copy.107), channel_id=1, source_target_pairs={{0,1},{1,2},{2,3},{3,4},{4,5},{5,6},{6,7},{7,8},{8,9},{9,10},{10,1... | collective-permute-start | bytes 442376 | tf_op jit(solution)/shard_map/ppermute | solution.py:15
  18.1 1.9 collective-permute-start.10
  20.1 7.9 %collective-permute-start.7 = (f32[4,4,256]{2,1,0:T(4,128)S(1)}, f32[4,4,256]{2,1,0:T(4,128)S(1)}, u32[]{:S(2)}, u32[]{:S(2)}) collective-permute-start(f32[4,4,256]{2,1,0:T(4,128)S(1)} %get-tuple-element.71), channel_id=1, source_target_pairs={{0,1},{1,2},{2,3},{3,4},{4,5},{5,6},{6,7},{7,8},{8,9},{9,10},{10,1... | collective-permute-start | bytes 49160 | tf_op jit(solution)/shard_map/ppermute | solution.py:15
  28.4 1.9 collective-permute-start.8
  31.0 1.9 collective-permute-start.4
  33.0 7.9 %collective-permute-start.5 = (f32[1,72,2,256]{3,1,2,0:T(8,128)S(1)}, f32[1,72,2,256]{3,1,2,0:T(8,128)S(1)}, u32[]{:S(2)}, u32[]{:S(2)}) collective-permute-start(f32[1,72,2,256]{3,1,2,0:T(8,128)S(1)} %get-tuple-element.47), channel_id=1, source_target_pairs={{0,1},{1,2},{2,3},{3,4},{4,5},{5,6},{6,7},{7,8},{8,9},{9,10},{10,1... | collective-permute-start | bytes 442376 | tf_op jit(solution)/shard_map/ppermute | solution.py:15
  41.8 2.6 %collective-permute-done.5 = f32[1,72,2,256]{3,1,2,0:T(8,128)S(1)} collective-permute-done((f32[1,72,2,256]{3,1,2,0:T(8,128)S(1)}, f32[1,72,2,256]{3,1,2,0:T(8,128)S(1)}, u32[]{:S(2)}, u32[]{:S(2)}) %collective-permute-start.5) | collective-permute-done | bytes 147488 | tf_op jit(solution)/shard_map/ppermute | solution.py:15
  45.7 8.6 %collective-permute-start.11 = (f32[1,72,2,256]{3,1,2,0:T(8,128)S(1)}, f32[1,72,2,256]{3,1,2,0:T(8,128)S(1)}, u32[]{:S(2)}, u32[]{:S(2)}) collective-permute-start(f32[1,72,2,256]{3,1,2,0:T(8,128)S(1)} %get-tuple-element.60), channel_id=1, source_target_pairs={{0,1},{1,2},{2,3},{3,4},{4,5},{5,6},{6,7},{7,8},{8,9},{9,10},{10,1... | collective-permute-start | bytes 442376 | tf_op jit(solution)/shard_map/ppermute | solution.py:15
  54.4 1.9 collective-permute-start.12
  56.5 10.1 %collective-permute-done.12 = f32[1,72,2,256]{3,1,2,0:T(8,128)S(1)} collective-permute-done((f32[1,72,2,256]{3,1,2,0:T(8,128)S(1)}, f32[1,72,2,256]{3,1,2,0:T(8,128)S(1)}, u32[]{:S(2)}, u32[]{:S(2)}) %collective-permute-start.12) | collective-permute-done | bytes 147488 | tf_op jit(solution)/shard_map/ppermute | solution.py:18
  67.1 1.9 collective-permute-start.13
  69.6 2.2 scatter_custom_fusion
  73.4 1.5 copy.63
  74.8 4.2 %collective-permute-start.6 = (f32[72,8,256]{2,0,1:T(8,128)S(1)}, f32[72,8,256]{2,0,1:T(8,128)S(1)}, u32[]{:S(2)}, u32[]{:S(2)}) collective-permute-start(f32[72,8,256]{2,0,1:T(8,128)S(1)} %get-tuple-element.73), channel_id=1, source_target_pairs={{0,64},{64,128},{128,192},{192,256},{256,320},{320,384},{384,448},... | collective-permute-start | bytes 1769480 | tf_op jit(solution)/shard_map/ppermute | solution.py:26
  79.1 6.2 %collective-permute-done.13 = f32[72,8,256]{2,0,1:T(8,128)} collective-permute-done((f32[72,8,256]{2,0,1:T(8,128)S(1)}, f32[72,8,256]{2,0,1:T(8,128)}, u32[]{:S(2)}, u32[]{:S(2)}) %collective-permute-start.13) | collective-permute-done | bytes 589856 | tf_op jit(solution)/shard_map/ppermute | solution.py:26
  85.3 1.5 broadcast_multiply_fusion.7
  86.7 1.9 collective-permute-start
  88.7 7.9 %collective-permute-start.1 = (f32[1,72,1,256]{3,1,2,0:T(8,128)S(1)}, f32[1,72,1,256]{3,1,2,0:T(8,128)S(1)}, u32[]{:S(2)}, u32[]{:S(2)}) collective-permute-start(f32[1,72,1,256]{3,1,2,0:T(8,128)S(1)} %get-tuple-element.57), channel_id=1, source_target_pairs={{0,1},{1,2},{2,3},{3,4},{4,5},{5,6},{6,7},{7,8},{8,9},{9,10},{10,1... | collective-permute-start | bytes 221192 | tf_op jit(solution)/shard_map/ppermute | solution.py:15
  97.9 1.2 fusion.93
  99.2 2.1 collective-permute-start.14
  101.3 24.9 %collective-permute-done.14 = f32[2,72,8,256]{3,1,2,0:T(8,128)} collective-permute-done((f32[2,72,8,256]{3,1,2,0:T(8,128)S(1)}, f32[2,72,8,256]{3,1,2,0:T(8,128)}, u32[]{:S(2)}, u32[]{:S(2)}) %collective-permute-start.14) | collective-permute-done | bytes 1179680 | tf_op jit(solution)/shard_map/ppermute | solution.py:26
  126.1 1.7 copy_select_fusion
  128.5 8.9 %collective-permute-start.23 = (f32[1,72,2,256]{3,1,2,0:T(8,128)S(1)}, f32[1,72,2,256]{3,1,2,0:T(8,128)S(1)}, u32[]{:S(2)}, u32[]{:S(2)}) collective-permute-start(f32[1,72,2,256]{3,1,2,0:T(8,128)S(1)} %get-tuple-element.22), channel_id=1, source_target_pairs={{0,1},{1,2},{2,3},{3,4},{4,5},{5,6},{6,7},{7,8},{8,9},{9,10},{10,1... | collective-permute-start | bytes 442376 | tf_op jit(solution)/shard_map/ppermute | solution.py:15
  137.5 1.9 collective-permute-start.24
  139.7 8.4 %collective-permute-done.24 = f32[1,72,2,256]{3,1,2,0:T(8,128)S(1)} collective-permute-done((f32[1,72,2,256]{3,1,2,0:T(8,128)S(1)}, f32[1,72,2,256]{3,1,2,0:T(8,128)S(1)}, u32[]{:S(2)}, u32[]{:S(2)}) %collective-permute-start.24) | collective-permute-done | bytes 147488 | tf_op jit(solution)/shard_map/ppermute | solution.py:18
  149.4 1.9 collective-permute-start.25
  151.3 2.4 %collective-permute-start.26 = (f32[1,72,2,256]{3,1,2,0:T(8,128)}, f32[1,72,2,256]{3,1,2,0:T(8,128)}, u32[]{:S(2)}, u32[]{:S(2)}) collective-permute-start(f32[1,72,2,256]{3,1,2,0:T(8,128)} %get-tuple-element.37), channel_id=1, source_target_pairs={{1,0},{2,1},{3,2},{4,3},{5,4},{6,5},{7,6},{8,7},{9,8},{10,9},{11,1... | collective-permute-start | bytes 442376 | tf_op jit(solution)/shard_map/ppermute | solution.py:18
  154.0 2.3 %gather_fusion = f32[256]{0:T(256)} fusion(f32[147456]{0:T(1024)S(1)} %bitcast.107, s32[1024]{0:T(1024)S(1)} %pad_clamp_fusion), kind=kCustom, calls=%fused_computation.clone | custom fusion | bytes 3072 | tf_op jit(solution)/shard_map/jit(_take)/gather | solution.py:97
  156.7 5.7 %collective-permute-done.26 = f32[1,72,2,256]{3,1,2,0:T(8,128)} collective-permute-done((f32[1,72,2,256]{3,1,2,0:T(8,128)}, f32[1,72,2,256]{3,1,2,0:T(8,128)}, u32[]{:S(2)}, u32[]{:S(2)}) %collective-permute-start.26) | collective-permute-done | bytes 147488 | tf_op jit(solution)/shard_map/ppermute | solution.py:18
  163.6 1.2 fusion.39
  164.8 1.9 collective-permute-start.27
  166.7 2.1 collective-permute-start.22
  168.8 9.2 %collective-permute-done.22 = f32[256]{0:T(256)S(1)} collective-permute-done((f32[256]{0:T(256)S(1)}, f32[256]{0:T(256)S(1)}, u32[]{:S(2)}, u32[]{:S(2)}) %collective-permute-start.22) | collective-permute-done | bytes 1056 | tf_op jit(solution)/shard_map/ppermute | solution.py:26
  178.7 2.2 scatter_custom_fusion.1
  182.0 1.9 collective-permute-start.17
  183.9 7.9 %collective-permute-start.18 = (f32[1,72,2,256]{3,1,2,0:T(8,128)S(1)}, f32[1,72,2,256]{3,1,2,0:T(8,128)S(1)}, u32[]{:S(2)}, u32[]{:S(2)}) collective-permute-start(f32[1,72,2,256]{3,1,2,0:T(8,128)S(1)} %copy-done.14), channel_id=1, source_target_pairs={{0,1},{1,2},{2,3},{3,4},{4,5},{5,6},{6,7},{7,8},{8,9},{9,10},{10,1... | collective-permute-start | bytes 442376 | tf_op jit(solution)/shard_map/ppermute | solution.py:15
  192.7 2.7 %collective-permute-done.18 = f32[1,72,2,256]{3,1,2,0:T(8,128)S(1)} collective-permute-done((f32[1,72,2,256]{3,1,2,0:T(8,128)S(1)}, f32[1,72,2,256]{3,1,2,0:T(8,128)S(1)}, u32[]{:S(2)}, u32[]{:S(2)}) %collective-permute-start.18) | collective-permute-done | bytes 147488 | tf_op jit(solution)/shard_map/ppermute | solution.py:15
  195.9 1.9 collective-permute-start.19
  197.9 8.7 %collective-permute-start.20 = (f32[1,72,2,256]{3,1,2,0:T(8,128)S(1)}, f32[1,72,2,256]{3,1,2,0:T(8,128)S(1)}, u32[]{:S(2)}, u32[]{:S(2)}) collective-permute-start(f32[1,72,2,256]{3,1,2,0:T(8,128)S(1)} %get-tuple-element.39), channel_id=1, source_target_pairs={{0,1},{1,2},{2,3},{3,4},{4,5},{5,6},{6,7},{7,8},{8,9},{9,10},{10,1... | collective-permute-start | bytes 442376 | tf_op jit(solution)/shard_map/ppermute | solution.py:15
  207.5 1.5 collective-permute-done.20
  210.1 3.7 %collective-permute-start.21 = (f32[72,8,256]{2,0,1:T(8,128)}, f32[72,8,256]{2,0,1:T(8,128)}, u32[]{:S(2)}, u32[]{:S(2)}) collective-permute-start(f32[72,8,256]{2,0,1:T(8,128)} %fusion.17), channel_id=1, source_target_pairs={{0,64},{64,128},{128,192},{192,256},{256,320},{320,384},{384,448},... | collective-permute-start | bytes 1769480 | tf_op jit(solution)/shard_map/ppermute | solution.py:26
  214.7 1.9 collective-permute-start.15
  216.7 8.9 %collective-permute-start.16 = (f32[1,72,1,256]{3,1,2,0:T(8,128)}, f32[1,72,1,256]{3,1,2,0:T(8,128)}, u32[]{:S(2)}, u32[]{:S(2)}) collective-permute-start(f32[1,72,1,256]{3,1,2,0:T(8,128)} %get-tuple-element.45), channel_id=1, source_target_pairs={{0,1},{1,2},{2,3},{3,4},{4,5},{5,6},{6,7},{7,8},{8,9},{9,10},{10,1... | collective-permute-start | bytes 221192 | tf_op jit(solution)/shard_map/ppermute | solution.py:15
  225.9 2.5 %gather_fusion.1 = f32[256]{0:T(256)} fusion(f32[147456]{0:T(1024)S(1)} %bitcast.106, s32[1024]{0:T(1024)} %copy-done.21), kind=kCustom, calls=%fused_computation.1.clone | custom fusion | bytes 3072 | tf_op jit(solution)/shard_map/jit(_take)/gather | solution.py:97
  230.6 2.2 fusion.60
  (156 shorter events, 21.3 us)
Async XLA Ops:
  0.6 27.3 %copy-start = (f32[1,72,8,256]{3,2,1,0:T(8,128)S(1)}, f32[1,72,8,256]{3,2,1,0:T(8,128)}, u32[]{:S(2)}) copy-start(f32[1,72,8,256]{3,2,1,0:T(8,128)} %param.15) | copy-start | bytes 1769476
  0.6 9.5 %copy-start.1 = (f32[1,72,8,256]{3,2,1,0:T(8,128)S(1)}, f32[1,72,8,256]{3,2,1,0:T(8,128)}, u32[]{:S(2)}) copy-start(f32[1,72,8,256]{3,2,1,0:T(8,128)} %param.13) | copy-start | bytes 1769476
  0.7 19.4 %copy-start.11 = (f32[3,8,256]{2,1,0:T(8,128)S(1)}, f32[3,8,256]{2,1,0:T(8,128)}, u32[]{:S(2)}) copy-start(f32[3,8,256]{2,1,0:T(8,128)} %param.21) | copy-start | bytes 73732
  2.2 26.2 %collective-permute-start.3 = (f32[1,72,2,256]{3,1,2,0:T(8,128)S(1)}, f32[1,72,2,256]{3,1,2,0:T(8,128)S(1)}, u32[]{:S(2)}, u32[]{:S(2)}) collective-permute-start(f32[1,72,2,256]{3,1,2,0:T(8,128)S(1)} %copy.109), channel_id=1, source_target_pairs={{0,1},{1,2},{2,3},{3,4},{4,5},{5,6},{6,7},{7,8},{8,9},{9,10},{10,1... | collective-permute-start | bytes 442376 | tf_op jit(solution)/shard_map/ppermute | solution.py:15
  8.2 22.4 %collective-permute-start.2 = (f32[1,72,2,256]{3,1,2,0:T(8,128)S(1)}, f32[1,72,2,256]{3,1,2,0:T(8,128)S(1)}, u32[]{:S(2)}, u32[]{:S(2)}) collective-permute-start(f32[1,72,2,256]{3,1,2,0:T(8,128)S(1)} %copy.110), channel_id=1, source_target_pairs={{1,0},{2,1},{3,2},{4,3},{5,4},{6,5},{7,6},{8,7},{9,8},{10,9},{11,1... | collective-permute-start | bytes 442376 | tf_op jit(solution)/shard_map/ppermute | solution.py:18
  10.2 30.8 %collective-permute-start.9 = (f32[1,72,2,256]{3,1,2,0:T(8,128)S(1)}, f32[1,72,2,256]{3,1,2,0:T(8,128)S(1)}, u32[]{:S(2)}, u32[]{:S(2)}) collective-permute-start(f32[1,72,2,256]{3,1,2,0:T(8,128)S(1)} %copy.107), channel_id=1, source_target_pairs={{0,1},{1,2},{2,3},{3,4},{4,5},{5,6},{6,7},{7,8},{8,9},{9,10},{10,1... | collective-permute-start | bytes 442376 | tf_op jit(solution)/shard_map/ppermute | solution.py:15
  18.1 27.0 %collective-permute-start.10 = (f32[1,72,2,256]{3,1,2,0:T(8,128)S(1)}, f32[1,72,2,256]{3,1,2,0:T(8,128)S(1)}, u32[]{:S(2)}, u32[]{:S(2)}) collective-permute-start(f32[1,72,2,256]{3,1,2,0:T(8,128)S(1)} %copy.108), channel_id=1, source_target_pairs={{1,0},{2,1},{3,2},{4,3},{5,4},{6,5},{7,6},{8,7},{9,8},{10,9},{11,1... | collective-permute-start | bytes 442376 | tf_op jit(solution)/shard_map/ppermute | solution.py:18
  20.1 12.9 %collective-permute-start.7 = (f32[4,4,256]{2,1,0:T(4,128)S(1)}, f32[4,4,256]{2,1,0:T(4,128)S(1)}, u32[]{:S(2)}, u32[]{:S(2)}) collective-permute-start(f32[4,4,256]{2,1,0:T(4,128)S(1)} %get-tuple-element.71), channel_id=1, source_target_pairs={{0,1},{1,2},{2,3},{3,4},{4,5},{5,6},{6,7},{7,8},{8,9},{9,10},{10,1... | collective-permute-start | bytes 49160 | tf_op jit(solution)/shard_map/ppermute | solution.py:15
  28.4 16.0 %copy-start.12 = (f32[8,256]{1,0:T(8,128)}, f32[8,256]{1,0:T(8,128)S(1)}, u32[]{:S(2)}) copy-start(f32[8,256]{1,0:T(8,128)S(1)} %get-tuple-element.69) | copy-start | bytes 24580
  28.4 12.4 %collective-permute-start.8 = (f32[4,4,256]{2,1,0:T(4,128)S(1)}, f32[4,4,256]{2,1,0:T(4,128)S(1)}, u32[]{:S(2)}, u32[]{:S(2)}) collective-permute-start(f32[4,4,256]{2,1,0:T(4,128)S(1)} %get-tuple-element.72), channel_id=1, source_target_pairs={{1,0},{2,1},{3,2},{4,3},{5,4},{6,5},{7,6},{8,7},{9,8},{10,9},{11,1... | collective-permute-start | bytes 49160 | tf_op jit(solution)/shard_map/ppermute | solution.py:18
  31.0 10.8 %collective-permute-start.4 = (f32[1,72,2,256]{3,1,2,0:T(8,128)S(1)}, f32[1,72,2,256]{3,1,2,0:T(8,128)S(1)}, u32[]{:S(2)}, u32[]{:S(2)}) collective-permute-start(f32[1,72,2,256]{3,1,2,0:T(8,128)S(1)} %get-tuple-element.46), channel_id=1, source_target_pairs={{1,0},{2,1},{3,2},{4,3},{5,4},{6,5},{7,6},{8,7},{9,8},{10,9},{11,1... | collective-permute-start | bytes 442376 | tf_op jit(solution)/shard_map/ppermute | solution.py:18
  33.0 11.4 %collective-permute-start.5 = (f32[1,72,2,256]{3,1,2,0:T(8,128)S(1)}, f32[1,72,2,256]{3,1,2,0:T(8,128)S(1)}, u32[]{:S(2)}, u32[]{:S(2)}) collective-permute-start(f32[1,72,2,256]{3,1,2,0:T(8,128)S(1)} %get-tuple-element.47), channel_id=1, source_target_pairs={{0,1},{1,2},{2,3},{3,4},{4,5},{5,6},{6,7},{7,8},{8,9},{9,10},{10,1... | collective-permute-start | bytes 442376 | tf_op jit(solution)/shard_map/ppermute | solution.py:15
  40.9 25.7 %copy-start.3 = (f32[12,256]{1,0:T(8,128)}, f32[12,256]{1,0:T(8,128)S(1)}, u32[]{:S(2)}) copy-start(f32[12,256]{1,0:T(8,128)S(1)} %get-tuple-element.66) | copy-start | bytes 36868
  40.9 25.7 %copy-start.6 = (f32[12,256]{1,0:T(8,128)}, f32[12,256]{1,0:T(8,128)S(1)}, u32[]{:S(2)}) copy-start(f32[12,256]{1,0:T(8,128)S(1)} %get-tuple-element.67) | copy-start | bytes 36868
  45.7 10.8 %collective-permute-start.11 = (f32[1,72,2,256]{3,1,2,0:T(8,128)S(1)}, f32[1,72,2,256]{3,1,2,0:T(8,128)S(1)}, u32[]{:S(2)}, u32[]{:S(2)}) collective-permute-start(f32[1,72,2,256]{3,1,2,0:T(8,128)S(1)} %get-tuple-element.60), channel_id=1, source_target_pairs={{0,1},{1,2},{2,3},{3,4},{4,5},{5,6},{6,7},{7,8},{8,9},{9,10},{10,1... | collective-permute-start | bytes 442376 | tf_op jit(solution)/shard_map/ppermute | solution.py:15
  54.4 12.2 %collective-permute-start.12 = (f32[1,72,2,256]{3,1,2,0:T(8,128)S(1)}, f32[1,72,2,256]{3,1,2,0:T(8,128)S(1)}, u32[]{:S(2)}, u32[]{:S(2)}) collective-permute-start(f32[1,72,2,256]{3,1,2,0:T(8,128)S(1)} %get-tuple-element.61), channel_id=1, source_target_pairs={{1,0},{2,1},{3,2},{4,3},{5,4},{6,5},{7,6},{8,7},{9,8},{10,9},{11,1... | collective-permute-start | bytes 442376 | tf_op jit(solution)/shard_map/ppermute | solution.py:18
  67.1 18.2 %collective-permute-start.13 = (f32[72,8,256]{2,0,1:T(8,128)S(1)}, f32[72,8,256]{2,0,1:T(8,128)}, u32[]{:S(2)}, u32[]{:S(2)}) collective-permute-start(f32[72,8,256]{2,0,1:T(8,128)S(1)} %fusion.68), channel_id=1, source_target_pairs={{64,0},{128,64},{192,128},{256,192},{320,256},{384,320},{448,384},... | collective-permute-start | bytes 1769480 | tf_op jit(solution)/shard_map/ppermute | solution.py:26
  74.8 22.1 %collective-permute-start.6 = (f32[72,8,256]{2,0,1:T(8,128)S(1)}, f32[72,8,256]{2,0,1:T(8,128)S(1)}, u32[]{:S(2)}, u32[]{:S(2)}) collective-permute-start(f32[72,8,256]{2,0,1:T(8,128)S(1)} %get-tuple-element.73), channel_id=1, source_target_pairs={{0,64},{64,128},{128,192},{192,256},{256,320},{320,384},{384,448},... | collective-permute-start | bytes 1769480 | tf_op jit(solution)/shard_map/ppermute | solution.py:26
  86.7 10.2 %collective-permute-start = (f32[1,72,1,256]{3,1,2,0:T(8,128)S(1)}, f32[1,72,1,256]{3,1,2,0:T(8,128)S(1)}, u32[]{:S(2)}, u32[]{:S(2)}) collective-permute-start(f32[1,72,1,256]{3,1,2,0:T(8,128)S(1)} %get-tuple-element.56), channel_id=1, source_target_pairs={{1,0},{2,1},{3,2},{4,3},{5,4},{6,5},{7,6},{8,7},{9,8},{10,9},{11,1... | collective-permute-start | bytes 221192 | tf_op jit(solution)/shard_map/ppermute | solution.py:18
  88.7 9.3 %collective-permute-start.1 = (f32[1,72,1,256]{3,1,2,0:T(8,128)S(1)}, f32[1,72,1,256]{3,1,2,0:T(8,128)S(1)}, u32[]{:S(2)}, u32[]{:S(2)}) collective-permute-start(f32[1,72,1,256]{3,1,2,0:T(8,128)S(1)} %get-tuple-element.57), channel_id=1, source_target_pairs={{0,1},{1,2},{2,3},{3,4},{4,5},{5,6},{6,7},{7,8},{8,9},{9,10},{10,1... | collective-permute-start | bytes 221192 | tf_op jit(solution)/shard_map/ppermute | solution.py:15
  99.1 27.0 %copy-start.2 = (f32[2,72,8,256]{3,2,1,0:T(8,128)S(1)}, f32[2,72,8,256]{3,2,1,0:T(8,128)}, u32[]{:S(2)}) copy-start(f32[2,72,8,256]{3,2,1,0:T(8,128)} %param.16) | copy-start | bytes 3538948
  99.2 26.9 %collective-permute-start.14 = (f32[2,72,8,256]{3,1,2,0:T(8,128)S(1)}, f32[2,72,8,256]{3,1,2,0:T(8,128)}, u32[]{:S(2)}, u32[]{:S(2)}) collective-permute-start(f32[2,72,8,256]{3,1,2,0:T(8,128)S(1)} %pad_maximum_fusion), channel_id=1, source_target_pairs={{64,0},{128,64},{192,128},{256,192},{320,256},{384,320},{448,384},... | collective-permute-start | bytes 3538952 | tf_op jit(solution)/shard_map/ppermute | solution.py:26
  128.5 11.2 %collective-permute-start.23 = (f32[1,72,2,256]{3,1,2,0:T(8,128)S(1)}, f32[1,72,2,256]{3,1,2,0:T(8,128)S(1)}, u32[]{:S(2)}, u32[]{:S(2)}) collective-permute-start(f32[1,72,2,256]{3,1,2,0:T(8,128)S(1)} %get-tuple-element.22), channel_id=1, source_target_pairs={{0,1},{1,2},{2,3},{3,4},{4,5},{5,6},{6,7},{7,8},{8,9},{9,10},{10,1... | collective-permute-start | bytes 442376 | tf_op jit(solution)/shard_map/ppermute | solution.py:15
  137.5 10.7 %collective-permute-start.24 = (f32[1,72,2,256]{3,1,2,0:T(8,128)S(1)}, f32[1,72,2,256]{3,1,2,0:T(8,128)S(1)}, u32[]{:S(2)}, u32[]{:S(2)}) collective-permute-start(f32[1,72,2,256]{3,1,2,0:T(8,128)S(1)} %get-tuple-element.23), channel_id=1, source_target_pairs={{1,0},{2,1},{3,2},{4,3},{5,4},{6,5},{7,6},{8,7},{9,8},{10,9},{11,1... | collective-permute-start | bytes 442376 | tf_op jit(solution)/shard_map/ppermute | solution.py:18
  139.5 8.7 %copy-start.4 = (f32[12,256]{1,0:T(8,128)S(1)}, f32[12,256]{1,0:T(8,128)}, u32[]{:S(2)}) copy-start(f32[12,256]{1,0:T(8,128)} %copy-done.3) | copy-start | bytes 36868
  139.5 8.7 %copy-start.7 = (f32[12,256]{1,0:T(8,128)S(1)}, f32[12,256]{1,0:T(8,128)}, u32[]{:S(2)}) copy-start(f32[12,256]{1,0:T(8,128)} %copy-done.6) | copy-start | bytes 36868
  148.6 5.4 %copy-start.26 = (s32[256]{0:T(256)S(1)}, s32[256]{0:T(256)}, u32[]{:S(2)}) copy-start(s32[256]{0:T(256)} %copy-done.25) | copy-start | bytes 3076
  149.4 7.3 %collective-permute-start.25 = (f32[1,72,2,256]{3,1,2,0:T(8,128)}, f32[1,72,2,256]{3,1,2,0:T(8,128)}, u32[]{:S(2)}, u32[]{:S(2)}) collective-permute-start(f32[1,72,2,256]{3,1,2,0:T(8,128)} %get-tuple-element.36), channel_id=1, source_target_pairs={{0,1},{1,2},{2,3},{3,4},{4,5},{5,6},{6,7},{7,8},{8,9},{9,10},{10,1... | collective-permute-start | bytes 442376 | tf_op jit(solution)/shard_map/ppermute | solution.py:15
  151.3 11.1 %collective-permute-start.26 = (f32[1,72,2,256]{3,1,2,0:T(8,128)}, f32[1,72,2,256]{3,1,2,0:T(8,128)}, u32[]{:S(2)}, u32[]{:S(2)}) collective-permute-start(f32[1,72,2,256]{3,1,2,0:T(8,128)} %get-tuple-element.37), channel_id=1, source_target_pairs={{1,0},{2,1},{3,2},{4,3},{5,4},{6,5},{7,6},{8,7},{9,8},{10,9},{11,1... | collective-permute-start | bytes 442376 | tf_op jit(solution)/shard_map/ppermute | solution.py:18
  156.4 6.0 %copy-start.5 = (f32[12,256]{1,0:T(8,128)S(1)}, f32[12,256]{1,0:T(8,128)}, u32[]{:S(2)}) copy-start(f32[12,256]{1,0:T(8,128)} %copy-done.3) | copy-start | bytes 36868
  156.4 6.0 %copy-start.8 = (f32[12,256]{1,0:T(8,128)S(1)}, f32[12,256]{1,0:T(8,128)}, u32[]{:S(2)}) copy-start(f32[12,256]{1,0:T(8,128)} %copy-done.6) | copy-start | bytes 36868
  163.5 3.2 %copy-start.19 = (s32[256]{0:T(256)S(1)}, s32[256]{0:T(256)}, u32[]{:S(2)}) copy-start(s32[256]{0:T(256)} %param.20) | copy-start | bytes 3076
  163.5 3.2 %copy-start.29 = (f32[256]{0:T(256)S(1)}, f32[256]{0:T(256)}, u32[]{:S(2)}) copy-start(f32[256]{0:T(256)} %gather_fusion) | copy-start | bytes 3076
  163.5 3.2 %copy-start.28 = (f32[256]{0:T(256)S(1)}, f32[256]{0:T(256)}, u32[]{:S(2)}) copy-start(f32[256]{0:T(256)} %param.19) | copy-start | bytes 3076
  163.6 3.2 %copy-start.31 = (f32[1,256]{1,0:T(1,128)S(1)}, f32[1,256]{1,0:T(1,128)}, u32[]{:S(2)}) copy-start(f32[1,256]{1,0:T(1,128)} %param.14) | copy-start | bytes 3076
  163.6 14.5 %copy-start.32 = (f32[256]{0:T(256)S(1)}, f32[256]{0:T(256)}, u32[]{:S(2)}) copy-start(f32[256]{0:T(256)} %param.17) | copy-start | bytes 3076
  164.8 27.0 %collective-permute-start.27 = (f32[72,8,256]{2,0,1:T(8,128)}, f32[72,8,256]{2,0,1:T(8,128)S(1)}, u32[]{:S(2)}, u32[]{:S(2)}) collective-permute-start(f32[72,8,256]{2,0,1:T(8,128)} %fusion.39), channel_id=1, source_target_pairs={{64,0},{128,64},{192,128},{256,192},{320,256},{384,320},{448,384},... | collective-permute-start | bytes 1769480 | tf_op jit(solution)/shard_map/ppermute | solution.py:26
  166.7 11.3 %collective-permute-start.22 = (f32[256]{0:T(256)S(1)}, f32[256]{0:T(256)S(1)}, u32[]{:S(2)}, u32[]{:S(2)}) collective-permute-start(f32[256]{0:T(256)S(1)} %bitcast.118), channel_id=1, source_target_pairs={{64,0},{128,64},{192,128},{256,192},{320,256},{384,320},{448,384},... | collective-permute-start | bytes 3080 | tf_op jit(solution)/shard_map/ppermute | solution.py:26
  181.1 2.8 %copy-start.14 = (f32[1,72,2,256]{3,1,2,0:T(8,128)S(1)}, f32[1,72,2,256]{3,1,2,0:T(8,128)}, u32[]{:S(2)}) copy-start(f32[1,72,2,256]{3,1,2,0:T(8,128)} %get-tuple-element.24) | copy-start | bytes 442372
  181.1 10.7 %copy-start.23 = (f32[1,72]{1,0:T(1,128)S(1)}, f32[1,72]{1,0:T(1,128)}, u32[]{:S(2)}) copy-start(f32[1,72]{1,0:T(1,128)} %param.18) | copy-start | bytes 868
  182.0 10.8 %collective-permute-start.17 = (f32[1,72,2,256]{3,1,2,0:T(8,128)S(1)}, f32[1,72,2,256]{3,1,2,0:T(8,128)S(1)}, u32[]{:S(2)}, u32[]{:S(2)}) collective-permute-start(f32[1,72,2,256]{3,1,2,0:T(8,128)S(1)} %copy-done.15), channel_id=1, source_target_pairs={{1,0},{2,1},{3,2},{4,3},{5,4},{6,5},{7,6},{8,7},{9,8},{10,9},{11,1... | collective-permute-start | bytes 442376 | tf_op jit(solution)/shard_map/ppermute | solution.py:18
  183.9 11.5 %copy-start.13 = (f32[8,256]{1,0:T(8,128)S(1)}, f32[8,256]{1,0:T(8,128)}, u32[]{:S(2)}) copy-start(f32[8,256]{1,0:T(8,128)} %copy-done.12) | copy-start | bytes 24580
  183.9 11.5 %collective-permute-start.18 = (f32[1,72,2,256]{3,1,2,0:T(8,128)S(1)}, f32[1,72,2,256]{3,1,2,0:T(8,128)S(1)}, u32[]{:S(2)}, u32[]{:S(2)}) collective-permute-start(f32[1,72,2,256]{3,1,2,0:T(8,128)S(1)} %copy-done.14), channel_id=1, source_target_pairs={{0,1},{1,2},{2,3},{3,4},{4,5},{5,6},{6,7},{7,8},{8,9},{9,10},{10,1... | collective-permute-start | bytes 442376 | tf_op jit(solution)/shard_map/ppermute | solution.py:15
  195.9 11.5 %collective-permute-start.19 = (f32[1,72,2,256]{3,1,2,0:T(8,128)S(1)}, f32[1,72,2,256]{3,1,2,0:T(8,128)S(1)}, u32[]{:S(2)}, u32[]{:S(2)}) collective-permute-start(f32[1,72,2,256]{3,1,2,0:T(8,128)S(1)} %get-tuple-element.38), channel_id=1, source_target_pairs={{1,0},{2,1},{3,2},{4,3},{5,4},{6,5},{7,6},{8,7},{9,8},{10,9},{11,1... | collective-permute-start | bytes 442376 | tf_op jit(solution)/shard_map/ppermute | solution.py:18
  197.9 11.1 %collective-permute-start.20 = (f32[1,72,2,256]{3,1,2,0:T(8,128)S(1)}, f32[1,72,2,256]{3,1,2,0:T(8,128)S(1)}, u32[]{:S(2)}, u32[]{:S(2)}) collective-permute-start(f32[1,72,2,256]{3,1,2,0:T(8,128)S(1)} %get-tuple-element.39), channel_id=1, source_target_pairs={{0,1},{1,2},{2,3},{3,4},{4,5},{5,6},{6,7},{7,8},{8,9},{9,10},{10,1... | collective-permute-start | bytes 442376 | tf_op jit(solution)/shard_map/ppermute | solution.py:15
  210.1 20.5 %collective-permute-start.21 = (f32[72,8,256]{2,0,1:T(8,128)}, f32[72,8,256]{2,0,1:T(8,128)}, u32[]{:S(2)}, u32[]{:S(2)}) collective-permute-start(f32[72,8,256]{2,0,1:T(8,128)} %fusion.17), channel_id=1, source_target_pairs={{0,64},{64,128},{128,192},{192,256},{256,320},{320,384},{384,448},... | collective-permute-start | bytes 1769480 | tf_op jit(solution)/shard_map/ppermute | solution.py:26
  214.7 15.9 %collective-permute-start.15 = (f32[1,72,1,256]{3,1,2,0:T(8,128)}, f32[1,72,1,256]{3,1,2,0:T(8,128)}, u32[]{:S(2)}, u32[]{:S(2)}) collective-permute-start(f32[1,72,1,256]{3,1,2,0:T(8,128)} %get-tuple-element.44), channel_id=1, source_target_pairs={{1,0},{2,1},{3,2},{4,3},{5,4},{6,5},{7,6},{8,7},{9,8},{10,9},{11,1... | collective-permute-start | bytes 221192 | tf_op jit(solution)/shard_map/ppermute | solution.py:18
  216.7 14.0 %collective-permute-start.16 = (f32[1,72,1,256]{3,1,2,0:T(8,128)}, f32[1,72,1,256]{3,1,2,0:T(8,128)}, u32[]{:S(2)}, u32[]{:S(2)}) collective-permute-start(f32[1,72,1,256]{3,1,2,0:T(8,128)} %get-tuple-element.45), channel_id=1, source_target_pairs={{0,1},{1,2},{2,3},{3,4},{4,5},{5,6},{6,7},{7,8},{8,9},{9,10},{10,1... | collective-permute-start | bytes 221192 | tf_op jit(solution)/shard_map/ppermute | solution.py:15
  (13 other events, 16.8 us)
where the time goes:
time: 235 us; the launch traced here: 234 us
  starting transfers between devices  120 us (51%)
  waiting for transfers between devices  74.3 us (32%)
  local copies, waits for them, and re-layouts  18.5 us (8%)
  other arithmetic  16.1 us (7%)
  matrix products  3.38 us (1%)
    ppermute x11, starting transfers between devices, extended(): lax.ppermute(lax.slice_in_dim(block, block.shape[dim] - width, None, axis...  82.3 us
    ppermute x6, waiting for transfers between devices, passed_along(): return lax.ppermute(block, axis, route)  40.2 us
    ppermute x11, waiting for transfers between devices, extended(): lax.ppermute(lax.slice_in_dim(block, 0, width, axis=dim), axis, backward)  26.3 us
    ppermute x11, starting transfers between devices, extended(): lax.ppermute(lax.slice_in_dim(block, 0, width, axis=dim), axis, backward)  21.6 us
    ppermute x6, starting transfers between devices, passed_along(): return lax.ppermute(block, axis, route)  16 us
    ppermute x11, waiting for transfers between devices, extended(): lax.ppermute(lax.slice_in_dim(block, block.shape[dim] - width, None, axis...  7.74 us
    unnamed x80, local copies, waits for them, and re-layouts  6.43 us
    gather x2, local copies, waits for them, and re-layouts, saddle(): p_mu = obs_var[None, :] * mult + jnp.take(flat, obs_idx, axis=1)  4.8 us
  transfers between devices with their start and end apart: 28, of which 13 were waited for; matrix products, arithmetic and copies ran while one was open for 9% of the time, Pallas kernels for 0%

commit v1 on v0

v1 whole, which is shorter than its diff:
```python
import jax
import jax.numpy as jnp
from jax import lax
from jax.experimental import pallas as pl
from jax.experimental.pallas import tpu as pltpu
from jax.sharding import PartitionSpec as P

MESH = pl.DeviceIdType.MESH
F32 = jnp.float32
BF16 = jnp.bfloat16
LB = 8
NC = 3
GROUP = 4
CHUNKED = ("LC", "LT", "LB", "XC", "XT", "XB", "A", "E", "P", "B", "PT", "PB", "QT", "QB", "OL", "OX")
SINGLE = ("CC", "CT", "CB", "AUX", "F0", "F1", "MU", "OO")
SLOT = {name: i * NC for i, name in enumerate(CHUNKED)}
SLOT.update({name: len(CHUNKED) * NC + i for i, name in enumerate(SINGLE)})
NSEM = len(CHUNKED) * NC + len(SINGLE)


def halves(v):
    high = v.astype(BF16)
    return high, (v - high.astype(F32)).astype(BF16)


def kernel(
    lam, mult, dx, fresh, fobs, sigma, ovar, oidx, coef, vert, pattern,
    out_lam, out_obs, out_dx,
    ring_l, ring_x, ring_p, ring_q, ring_c, cen,
    a_buf, a_in, e_buf, e_in, m_buf, n_buf, b_buf, b_in, d2_in, dl, ht, ol_buf, ox_buf,
    aux, aux_in, mu_buf, mu_in, oo_buf, v3, onehot, ssem, rsem,
):
    levels, rows, cols = a_buf.shape
    nobs = oo_buf.shape[1]
    tms, sps = lax.axis_size("tm"), lax.axis_size("space")
    tm, sp = lax.axis_index("tm"), lax.axis_index("space")
    yl, c = lax.rem(tm, 2), lax.rem(sp, 2)
    rk, rt = tm - yl + c, sp - c + yl
    swapped = yl != c

    def at_role(k, t):
        kb, tb = lax.rem(k + 2, 2), lax.rem(t + 2, 2)
        return (k - kb + tb, t - tb + kb)

    partner = at_role(tm, sp)
    not_first_t, not_last_t = rt > 0, rt < sps - 1
    not_first_k, not_last_k = rk > 0, rk < tms - 1
    fresh_out = jnp.logical_and(tm == tms - 2, c == 0)
    fresh_far = jnp.logical_and(tm == tms - 2, c == 1)
    fresh_own = jnp.logical_and(tm == tms - 1, c == 1)
    links = {
        "swap": (partner, swapped, partner, swapped),
        "araw_top": (at_role(tm, sp - 1), sp > 0, (rk, rt + 1), not_last_t),
        "araw_bot": (at_role(tm, sp + 1), sp < sps - 1, (rk, rt - 1), not_first_t),
        "top": (at_role(rk, rt - 1), not_first_t, at_role(rk, rt + 1), not_last_t),
        "bot": (at_role(rk, rt + 1), not_last_t, at_role(rk, rt - 1), not_first_t),
        "down": (at_role(rk - 1, rt), not_first_k, at_role(rk + 1, rt), not_last_k),
        "fresh": ((tm, sp + 1), fresh_out, (tm, sp - 1), fresh_far),
    }

    barrier = pltpu.get_barrier_semaphore()
    for target, sends, source, receives in links.values():
        @pl.when(receives)
        def _():
            pl.semaphore_signal(barrier, inc=1, device_id=source, device_id_type=MESH)

    def remote(link, slot, src, dst):
        return pltpu.make_async_remote_copy(
            src_ref=src, dst_ref=dst, send_sem=ssem.at[slot], recv_sem=rsem.at[slot],
            device_id=links[link][0], device_id_type=MESH,
        )

    def start(link, slot, src, dst):
        @pl.when(links[link][1])
        def _():
            remote(link, slot, src, dst).start()

    def sent(link, slot, src, dst):
        @pl.when(links[link][1])
        def _():
            remote(link, slot, src, dst).wait_send()

    def arrive(link, slot, src, dst):
        @pl.when(links[link][3])
        def _():
            remote(link, slot, src, dst).wait_recv()

    def home(slot, src, dst, op):
        @pl.when(jnp.logical_not(swapped))
        def _():
            getattr(pltpu.make_async_copy(src, dst, rsem.at[slot]), op)()

    size = levels // NC

    def part(i):
        return pl.ds(i * size, size)

    top, bottom = pl.ds(0, rows // 2), pl.ds(rows // 2, rows // 2)
    center, below, above = pl.ds(0, rows), pl.ds(rows, rows // 2), pl.ds(rows + rows // 2, rows // 2)

    def raw_flows(prefix, array, ring, span, slot):
        return (
            ("swap", slot(prefix + "C"), array.at[span], ring.at[span, center]),
            ("araw_top", slot(prefix + "T"), array.at[span, top], ring.at[span, below]),
            ("araw_bot", slot(prefix + "B"), array.at[span, bottom], ring.at[span, above]),
        )

    def raw_start(flows):
        for flow in flows:
            start(*flow)
        home(*flows[0][1:], "start")

    def raw_wait(flows):
        for flow in flows:
            arrive(*flow)
        home(*flows[0][1:], "wait")

    flows_c = raw_flows("C", coef, ring_c, pl.ds(0, 3), lambda n: SLOT[n])
    flows_l = [raw_flows("L", lam, ring_l, part(i), lambda n, i=i: SLOT[n] + i) for i in range(NC)]
    flows_x = [raw_flows("X", dx, ring_x, part(i), lambda n, i=i: SLOT[n] + i) for i in range(NC)]

    def halo_flows(prefix, ring):
        return [
            (
                ("top", SLOT[prefix + "T"] + i, ring.at[part(i), top], ring.at[part(i), below]),
                ("bot", SLOT[prefix + "B"] + i, ring.at[part(i), bottom], ring.at[part(i), above]),
            )
            for i in range(NC)
        ]

    halo_p, halo_q = halo_flows("P", ring_p), halo_flows("Q", ring_q)
    down_a = [("down", SLOT["A"] + i, a_buf.at[part(i)], a_in.at[part(i)]) for i in range(NC)]
    down_e = [("down", SLOT["E"] + i, e_buf.at[part(i)], e_in.at[part(i)]) for i in range(NC)]
    down_p = [("down", SLOT["P"] + i, ring_p.at[part(i), center], d2_in.at[part(i)]) for i in range(NC)]
    down_b = [("down", SLOT["B"] + i, b_buf.at[part(i)], b_in.at[part(i)]) for i in range(NC)]
    down_mu = ("down", SLOT["MU"], mu_buf, mu_in)
    flow_aux = ("swap", SLOT["AUX"], aux, aux_in)
    fresh_0 = ("fresh", SLOT["F0"], fresh.at[0], e_in)
    fresh_1 = ("fresh", SLOT["F1"], fresh.at[1], d2_in)
    out_l = [("swap", SLOT["OL"] + i, ol_buf.at[part(i)], out_lam.at[part(i)]) for i in range(NC)]
    out_x = [("swap", SLOT["OX"] + i, ox_buf.at[part(i)], out_dx.at[part(i)]) for i in range(NC)]
    out_o = ("swap", SLOT["OO"], oo_buf, out_obs)

    rings = (ring_l, ring_x, ring_p, ring_q, ring_c)

    @pl.when(jnp.logical_not(not_first_t))
    def _():
        for ring in rings:
            ring[:, rows + rows // 2:, :] = jnp.zeros((ring.shape[0], rows // 2, cols), F32)

    @pl.when(jnp.logical_not(not_last_t))
    def _():
        for ring in rings:
            ring[:, rows:rows + rows // 2, :] = jnp.zeros((ring.shape[0], rows // 2, cols), F32)

    @pl.when(jnp.logical_not(not_last_k))
    def _():
        a_in[...] = jnp.zeros(a_in.shape, F32)
        b_in[...] = jnp.zeros(b_in.shape, F32)

    aux[...] = jnp.zeros(aux.shape, F32)
    aux[0:1, :] = mult[...]
    aux[1:2, :] = fobs[...]
    aux[2:3, :] = ovar[...]
    aux[3:4, :] = oidx[...].astype(F32)
    aux[4:5, 0:levels] = sigma[...]

    pl.semaphore_wait(barrier, sum(link[1].astype(jnp.int32) for link in links.values()))

    raw_start(flows_c)
    start(*flow_aux)
    for i in range(NC):
        raw_start(flows_l[i])
    start(*fresh_0)
    start(*fresh_1)

    @pl.when(fresh_own)
    def _():
        pltpu.make_async_copy(fresh.at[0], e_in, rsem.at[SLOT["F0"]]).start()
        pltpu.make_async_copy(fresh.at[1], d2_in, rsem.at[SLOT["F1"]]).start()

    @pl.when(jnp.logical_not(swapped))
    def _():
        aux_in[...] = aux[...]

    arrive(*flow_aux)
    index = aux_in[3:4, :].astype(jnp.int32)
    row_of, col_of = index // cols, index % cols
    onehot[...] = jnp.where(
        lax.broadcasted_iota(jnp.int32, (levels * rows, nobs), 0) == row_of, 1.0, 0.0
    ).astype(BF16)
    mu = aux_in[0:1, :]
    var = aux_in[2:3, :]
    at_col = lax.broadcasted_iota(jnp.int32, (cols, nobs), 0) == col_of

    def spread(weights):
        high, low = halves(jnp.where(at_col, weights, 0.0))
        nt = (((1,), (1,)), ((), ()))
        total = lax.dot_general(onehot[...], high, nt, preferred_element_type=F32)
        total += lax.dot_general(onehot[...], low, nt, preferred_element_type=F32)
        ht[...] = total.reshape(ht.shape)

    def sampled(field):
        high, low = halves(field.reshape(levels * rows, cols))
        tn = (((0,), (0,)), ((), ()))
        total = lax.dot_general(high, onehot[...], tn, preferred_element_type=F32)
        total += lax.dot_general(low, onehot[...], tn, preferred_element_type=F32)
        return jnp.sum(jnp.where(at_col, total, 0.0), axis=0, keepdims=True)

    spread(mu)

    square = (levels, levels)
    lev_i = lax.broadcasted_iota(jnp.int32, square, 0)
    lev_j = lax.broadcasted_iota(jnp.int32, square, 1)
    nb = pattern.shape[0]
    wide = (
        lax.broadcasted_iota(jnp.int32, (levels, nb), 0) // LB
        == lax.broadcasted_iota(jnp.int32, (levels, nb), 1)
    ).astype(F32)
    keep = lax.dot_general(
        jnp.dot(wide, pattern[...].astype(F32), preferred_element_type=F32),
        wide, (((1,), (1,)), ((), ())), preferred_element_type=F32,
    )
    keep = jnp.maximum(keep, (lev_i // LB == lev_j // LB).astype(F32))
    eye = (lev_i == lev_j).astype(F32)
    sig_row = aux_in[4:5, 0:levels]
    sig_col = jnp.sum(eye * sig_row, axis=1, keepdims=True)
    v_high, v_low = halves(sig_col * (2.0 * eye + keep * vert[...]) * sig_row)
    deep = v3.shape[1] // 3
    pick_i = lax.broadcasted_iota(jnp.int32, (levels, 3 * deep), 0)
    pick_j = lax.broadcasted_iota(jnp.int32, (levels, 3 * deep), 1)
    first_two = jnp.logical_or(pick_j == pick_i, pick_j == pick_i + deep).astype(BF16)
    third = (pick_j == pick_i + 2 * deep).astype(BF16)
    v3[...] = (
        jnp.dot(v_high, first_two, preferred_element_type=F32)
        + jnp.dot(v_low, third, preferred_element_type=F32)
    ).astype(BF16)

    def vertical(ring, write):
        pad = jnp.zeros((deep - levels, cols), F32)
        for y in range(rows):
            def row(r):
                return ring[:, (r + 2 * rows) % (2 * rows), :]
            mid = row(y)
            smooth = 0.6 * mid + 0.1 * (
                row(y - 1) + row(y + 1) + pltpu.roll(mid, 1, 1) + pltpu.roll(mid, cols - 1, 1)
            )
            high, low = halves(jnp.concatenate([smooth, pad], axis=0))
            stack = jnp.concatenate([high, low, high], axis=0)
            write(y, jnp.dot(v3[...], stack, preferred_element_type=F32))

    def store_dl(y, value):
        dl[:, y, :] = value

    raw_wait(flows_c)
    cen[...] = 1.0 - 2.0 * ring_c[0] - 2.0 * ring_c[1] - ring_c[2]
    rid = lax.broadcasted_iota(jnp.int32, (rows, cols), 0)
    inside = jnp.where(rid < rows // 2, not_last_t.astype(F32), not_first_t.astype(F32))

    def shifted(own, other, s):
        wrap = rid < s if s > 0 else rid >= rows + s
        return jnp.where(wrap, pltpu.roll(other, s % rows, 0), pltpu.roll(own, s % rows, 0))

    def tl_tile(own, other, rs):
        near = shifted(own, other, 1) + shifted(own, other, -1)
        far = shifted(own, other, 2) + shifted(own, other, -2)
        return (
            cen[rs, :] * own + ring_c[0, rs, :] * near + ring_c[1, rs, :] * far
            + ring_c[2, rs, :] * pltpu.roll(own, 1, 1)
        )

    main, side = pl.ds(0, rows), pl.ds(rows, rows)

    def tl_model(ring, l):
        own, other = ring[l, 0:rows, :], ring[l, rows:, :]
        first, second = tl_tile(own, other, main), tl_tile(other, own, side)
        return tl_tile(first, second, main)

    def ad_tile(own, other, p, p2, r, r2, rs):
        return (
            cen[rs, :] * own + (shifted(p, p2, 1) + shifted(p, p2, -1))
            + (shifted(r, r2, 2) + shifted(r, r2, -2))
            + pltpu.roll(ring_c[2, rs, :] * own, cols - 1, 1)
        )

    def ad_model(ring, l):
        own, other = ring[l, 0:rows, :], ring[l, rows:, :]
        for step in range(2):
            p, p2 = ring_c[0, main, :] * own, ring_c[0, side, :] * other
            r, r2 = ring_c[1, main, :] * own, ring_c[1, side, :] * other
            new = ad_tile(own, other, p, p2, r, r2, main)
            if step == 0:
                other = ad_tile(other, own, p2, p, r2, r, side) * inside
            own = new
        return own

    def for_levels(i, body):
        def some(g, carry):
            for u in range(GROUP):
                body(i * size + g * GROUP + u)
            return carry
        lax.fori_loop(0, size // GROUP, some, 0)

    for i in range(NC):
        raw_wait(flows_l[i])
        raw_start(flows_x[i])

        def body(l):
            a_buf[l] = ad_model(ring_l, l)
        for_levels(i, body)
        start(*down_a[i])

    for i in range(NC):
        arrive(*down_a[i])

        def body(l):
            ring_p[l, 0:rows, :] = ring_l[l, 0:rows, :] - a_in[l] + ht[l]
        for_levels(i, body)
        for flow in halo_p[i]:
            start(*flow)
        start(*down_p[i])

    vertical(ring_l, store_dl)

    for i in range(NC):
        raw_wait(flows_x[i])

        def body(l):
            e_buf[l] = dl[l] + ring_x[l, 0:rows, :]
        for_levels(i, body)
        start(*down_e[i])

        def body(l):
            m_buf[l] = tl_model(ring_x, l)
        for_levels(i, body)

    mu_buf[...] = jnp.broadcast_to(var * mu + sampled(ring_x[:, 0:rows, :]), mu_buf.shape)
    start(*down_mu)

    arrive(*fresh_0)
    arrive(*fresh_1)

    @pl.when(fresh_own)
    def _():
        pltpu.make_async_copy(fresh.at[0], e_in, rsem.at[SLOT["F0"]]).wait()
        pltpu.make_async_copy(fresh.at[1], d2_in, rsem.at[SLOT["F1"]]).wait()

    @pl.when(jnp.logical_not(not_last_k))
    def _():
        mu_in[...] = jnp.broadcast_to(aux_in[1:2, :], mu_in.shape)
        m_buf[...] = jnp.zeros(m_buf.shape, F32)

    for i in range(NC):
        arrive(*down_e[i])

        def body(l):
            ring_q[l, 0:rows, :] = e_in[l] - m_buf[l]
        for_levels(i, body)
        for flow in halo_q[i]:
            start(*flow)

    keep_tl = not_first_k.astype(F32)
    for i in range(NC):
        for flow in halo_p[i]:
            arrive(*flow)
        arrive(*down_p[i])

        def body(l):
            n_buf[l] = d2_in[l] - keep_tl * tl_model(ring_p, l)
        for_levels(i, body)

    for i in range(NC):
        for flow in halo_q[i]:
            arrive(*flow)

        def body(l):
            b_buf[l] = ad_model(ring_q, l)
        for_levels(i, body)
        start(*down_b[i])

    vertical(ring_q, store_dl)
    for i in range(NC):
        def body(l):
            ol_buf[l] = dl[l] + n_buf[l]
        for_levels(i, body)
        start(*out_l[i])
        home(*out_l[i][1:], "start")

    arrive(*down_mu)
    mu_two = mu_in[0:1, :]
    oo_buf[...] = var * mu_two + sampled(d2_in[...])
    start(*out_o)

    @pl.when(jnp.logical_not(swapped))
    def _():
        out_obs[...] = oo_buf[...]

    spread(mu_two)
    for i in range(NC):
        arrive(*down_b[i])

        def body(l):
            ox_buf[l] = ring_q[l, 0:rows, :] - b_in[l] + ht[l]
        for_levels(i, body)
        start(*out_x[i])
        home(*out_x[i][1:], "start")

    everything = [flow_aux, fresh_0, fresh_1, down_mu, out_o, *flows_c]
    for group in (*flows_l, *flows_x, *halo_p, *halo_q):
        everything += list(group)
    everything += down_a + down_e + down_p + down_b + out_l + out_x
    for flow in everything:
        sent(*flow)
    for flow in (*out_l, *out_x):
        arrive(*flow)
        home(*flow[1:], "wait")
    arrive(*out_o)


def local(
    lam,
    obs_mult,
    dx,
    fresh_state,
    fresh_obs,
    sigma,
    obs_var,
    obs_idx,
    stencil_coef,
    vert_cov,
    block_pattern,
):
    field = dx.shape[1:]
    levels, rows, cols = field
    nobs = obs_mult.shape[1]
    ring = (levels, 2 * rows, cols)
    deep = -(-levels // 16) * 16
    anywhere, vmem = pl.BlockSpec(memory_space=pl.ANY), pl.BlockSpec(memory_space=pltpu.VMEM)
    out_lam, out_obs, out_dx = pl.pallas_call(
        kernel,
        name="saddle_slide",
        out_shape=(
            jax.ShapeDtypeStruct(field, F32),
            jax.ShapeDtypeStruct((1, nobs), F32),
            jax.ShapeDtypeStruct(field, F32),
        ),
        in_specs=[anywhere, vmem, anywhere, anywhere, vmem, vmem, vmem, vmem, anywhere, vmem, vmem],
        out_specs=(anywhere, vmem, anywhere),
        scratch_shapes=[
            *[pltpu.VMEM(ring, F32)] * 4,
            pltpu.VMEM((3, 2 * rows, cols), F32),
            pltpu.VMEM((2 * rows, cols), F32),
            *[pltpu.VMEM(field, F32)] * 13,
            pltpu.VMEM((8, nobs), F32),
            pltpu.VMEM((8, nobs), F32),
            pltpu.VMEM((8, nobs), F32),
            pltpu.VMEM((8, nobs), F32),
            pltpu.VMEM((1, nobs), F32),
            pltpu.VMEM((levels, 3 * deep), BF16),
            pltpu.VMEM((levels * rows, nobs), BF16),
            pltpu.SemaphoreType.DMA((NSEM,)),
            pltpu.SemaphoreType.DMA((NSEM,)),
        ],
        compiler_params=pltpu.CompilerParams(
            collective_id=0, has_side_effects=True, vmem_limit_bytes=48 * 2**20
        ),
        cost_estimate=pl.CostEstimate(flops=10**9, bytes_accessed=5 * 10**6, transcendentals=0),
    )(
        lam[0],
        obs_mult,
        dx[0],
        fresh_state,
        fresh_obs[None],
        sigma,
        obs_var[None],
        obs_idx[None],
        stencil_coef,
        vert_cov,
        block_pattern,
    )
    return out_lam[None], out_obs, out_dx[None]


def solution(mesh):
    in_specs = (
        P("tm", None, "space", None),
        P("tm", "space"),
        P("tm", None, "space", None),
        P(None, None, "space", None),
        P("space"),
        P("tm", None),
        P("space"),
        P("space"),
        P(None, "space", None),
        P(),
        P(),
    )
    out_specs = (P("tm", None, "space", None), P("tm", "space"), P("tm", None, "space", None))
    return jax.shard_map(local, mesh=mesh, in_specs=in_specs, out_specs=out_specs, check_vma=False)
```

time: 235 us -> 81.1 us (0.35)
  the two profiles are of different devices: /device:TPU:253 before, /device:TPU:1 now
where the time goes in v1:
time: 81.1 us; the launch traced here: 80.7 us
  Pallas kernels  68.8 us (85%)
  local copies, waits for them, and re-layouts  11.2 us (14%)
    pallas_call x1, Pallas kernels, local(): pl.pallas_call(kernel, name='saddle_slide', out_shape=(jax.ShapeDtypeStru...  68.8 us
    unnamed x25, local copies, waits for them, and re-layouts  11.2 us

profile of v1, /device:TPU:1, one launch (start us, length us, event | category | flops | bytes accessed | tf_op | source)
XLA Modules:
  0.0 80.7 jit_solution(3347369859788879968)
XLA Ops:
  0.6 0.0 copy-start
  0.6 1.3 %copy-done = f32[2,72,8,256]{3,2,1,0:T(8,128)S(1)} copy-done((f32[2,72,8,256]{3,2,1,0:T(8,128)S(1)}, f32[2,72,8,256]{3,2,1,0:T(8,128)}, u32[]{:S(2)}) %copy-start) | copy-done | bytes 1179672
  1.9 0.0 copy-start.1
  1.9 1.1 %copy-done.1 = f32[1,72,8,256]{3,2,1,0:T(8,128)S(1)} copy-done((f32[1,72,8,256]{3,2,1,0:T(8,128)S(1)}, f32[1,72,8,256]{3,2,1,0:T(8,128)}, u32[]{:S(2)}) %copy-start.1) | copy-done | bytes 589848
  3.0 0.0 copy-start.2
  3.0 1.1 %copy-done.2 = f32[1,72,8,256]{3,2,1,0:T(8,128)S(1)} copy-done((f32[1,72,8,256]{3,2,1,0:T(8,128)S(1)}, f32[1,72,8,256]{3,2,1,0:T(8,128)}, u32[]{:S(2)}) %copy-start.2) | copy-done | bytes 589848
  4.0 0.0 copy-start.3
  4.0 0.8 copy-done.3
  4.8 0.0 copy-start.4
  4.8 0.7 copy-done.4
  5.5 0.0 copy-start.5
  5.5 0.7 copy-done.5
  6.2 0.0 copy-start.6
  6.2 0.7 copy-done.6
  6.9 0.0 copy-start.7
  6.9 0.7 copy-done.7
  7.6 0.0 copy-start.8
  7.6 0.7 copy-done.8
  8.3 0.0 copy-start.9
  8.3 0.7 copy-done.9
  9.0 0.0 copy-start.10
  9.0 0.7 copy-done.10
  9.6 68.8 %saddle_slide.1 = (f32[72,8,256]{2,1,0:T(8,128)S(1)}, f32[1,256]{1,0:T(1,128)S(1)}, f32[72,8,256]{2,1,0:T(8,128)S(1)}) custom-call(f32[72,8,256]{2,1,0:T(8,128)S(1)} %bitcast.9, f32[1,256]{1,0:T(1,128)S(1)} %copy-done.6, f32[72,8,256]{2,1,0:T(8,128)S(1)} %bitcast.10, f32[2,72,8,256]{3,2,1,0:T(8,128)S(1)} %copy-done, f32[1,256]{1,0:T(1,128)S(1)} %bitcast.11, ...), custom_call_target="tpu_custom_call" | custom-call | flops 1000000000 | bytes 5000000 | tf_op jit(solution)/shard_map/saddle_slide/pallas_call | solution.py:439
  78.5 0.8 %copy.17 = f32[1,72,8,256]{3,2,1,0:T(8,128)} copy(f32[1,72,8,256]{3,2,1,0:T(8,128)S(1)} %bitcast.8) | data formatting | bytes 1179648
  79.3 0.6 copy.18
  79.8 0.8 %copy.19 = f32[1,72,8,256]{3,2,1,0:T(8,128)} copy(f32[1,72,8,256]{3,2,1,0:T(8,128)S(1)} %bitcast.7) | data formatting | bytes 1179648
Async XLA Ops:
  0.6 1.3 %copy-start = (f32[2,72,8,256]{3,2,1,0:T(8,128)S(1)}, f32[2,72,8,256]{3,2,1,0:T(8,128)}, u32[]{:S(2)}) copy-start(f32[2,72,8,256]{3,2,1,0:T(8,128)} %fresh.1) | copy-start | bytes 3538948
  1.9 1.1 %copy-start.1 = (f32[1,72,8,256]{3,2,1,0:T(8,128)S(1)}, f32[1,72,8,256]{3,2,1,0:T(8,128)}, u32[]{:S(2)}) copy-start(f32[1,72,8,256]{3,2,1,0:T(8,128)} %param.11) | copy-start | bytes 1769476
  3.0 1.1 %copy-start.2 = (f32[1,72,8,256]{3,2,1,0:T(8,128)S(1)}, f32[1,72,8,256]{3,2,1,0:T(8,128)}, u32[]{:S(2)}) copy-start(f32[1,72,8,256]{3,2,1,0:T(8,128)} %param.13) | copy-start | bytes 1769476
  4.0 0.8 copy-start.3
  4.8 0.7 copy-start.4
  5.5 0.7 copy-start.5
  6.2 0.7 copy-start.6
  6.9 0.7 copy-start.7
  7.6 0.7 copy-start.8
  8.3 0.7 copy-start.9
  9.0 0.7 copy-start.10

commit v2 on v1

--- a/solution.py
+++ b/solution.py
@@ -11,7 +11,7 @@
 LB = 8
 NC = 3
 GROUP = 4
-CHUNKED = ("LC", "LT", "LB", "XC", "XT", "XB", "A", "E", "P", "B", "PT", "PB", "QT", "QB", "OL", "OX")
+CHUNKED = ("LC", "LT", "LB", "XC", "XT", "XB", "A", "E", "P", "B", "PT", "PB", "QT", "QB", "OL", "OX", "LF", "XF")
 SINGLE = ("CC", "CT", "CB", "AUX", "F0", "F1", "MU", "OO")
 SLOT = {name: i * NC for i, name in enumerate(CHUNKED)}
 SLOT.update({name: len(CHUNKED) * NC + i for i, name in enumerate(SINGLE)})
@@ -24,12 +24,22 @@
 
 
 def kernel(
-    lam, mult, dx, fresh, fobs, sigma, ovar, oidx, coef, vert, pattern,
+    lam, mult_hbm, dx, fresh, fobs_hbm, sigma_hbm, ovar_hbm, oidx_hbm, coef, vert_hbm, pattern_hbm,
     out_lam, out_obs, out_dx,
     ring_l, ring_x, ring_p, ring_q, ring_c, cen,
     a_buf, a_in, e_buf, e_in, m_buf, n_buf, b_buf, b_in, d2_in, dl, ht, ol_buf, ox_buf,
-    aux, aux_in, mu_buf, mu_in, oo_buf, v3, onehot, ssem, rsem,
+    aux, aux_in, mu_buf, mu_in, oo_buf, v3, onehot,
+    mult, fobs, sigma, ovar, oidx, vert, pattern, ssem, rsem, fsem,
 ):
+    fetches = [
+        pltpu.make_async_copy(src, dst, fsem.at[i])
+        for i, (src, dst) in enumerate((
+            (mult_hbm, mult), (fobs_hbm, fobs), (sigma_hbm, sigma), (ovar_hbm, ovar), (oidx_hbm, oidx),
+            (vert_hbm, vert), (pattern_hbm, pattern),
+        ))
+    ]
+    for fetch in fetches:
+        fetch.start()
     levels, rows, cols = a_buf.shape
     nobs = oo_buf.shape[1]
     tms, sps = lax.axis_size("tm"), lax.axis_size("space")
@@ -48,6 +58,9 @@
     fresh_out = jnp.logical_and(tm == tms - 2, c == 0)
     fresh_far = jnp.logical_and(tm == tms - 2, c == 1)
     fresh_own = jnp.logical_and(tm == tms - 1, c == 1)
+    left_top = jnp.logical_and(yl == 1, c == 0)
+    left_bot = jnp.logical_and(yl == 0, c == 1)
+    high_high, low_low = jnp.logical_and(yl == 1, c == 1), jnp.logical_and(yl == 0, c == 0)
     links = {
         "swap": (partner, swapped, partner, swapped),
         "araw_top": (at_role(tm, sp - 1), sp > 0, (rk, rt + 1), not_last_t),
@@ -57,9 +70,19 @@
         "down": (at_role(rk - 1, rt), not_first_k, at_role(rk + 1, rt), not_last_k),
         "fresh": ((tm, sp + 1), fresh_out, (tm, sp - 1), fresh_far),
     }
+    peers = tuple(links.values())
+
+    def narrowed(name, sends, receives):
+        target, may_send, source, may_receive = links[name]
+        return (target, jnp.logical_and(may_send, sends), source, jnp.logical_and(may_receive, receives))
+
+    links["own_top"] = narrowed("araw_top", jnp.logical_not(left_top), jnp.logical_not(high_high))
+    links["own_bot"] = narrowed("araw_bot", jnp.logical_not(left_bot), jnp.logical_not(low_low))
+    links["on_top"] = narrowed("top", left_bot, high_high)
+    links["on_bot"] = narrowed("bot", left_top, low_low)
 
     barrier = pltpu.get_barrier_semaphore()
-    for target, sends, source, receives in links.values():
+    for target, sends, source, receives in peers:
         @pl.when(receives)
         def _():
             pl.semaphore_signal(barrier, inc=1, device_id=source, device_id_type=MESH)
@@ -98,11 +121,11 @@
     top, bottom = pl.ds(0, rows // 2), pl.ds(rows // 2, rows // 2)
     center, below, above = pl.ds(0, rows), pl.ds(rows, rows // 2), pl.ds(rows + rows // 2, rows // 2)
 
-    def raw_flows(prefix, array, ring, span, slot):
+    def raw_flows(prefix, array, ring, span, links, i=0):
         return (
-            ("swap", slot(prefix + "C"), array.at[span], ring.at[span, center]),
-            ("araw_top", slot(prefix + "T"), array.at[span, top], ring.at[span, below]),
-            ("araw_bot", slot(prefix + "B"), array.at[span, bottom], ring.at[span, above]),
+            ("swap", SLOT[prefix + "C"] + i, array.at[span], ring.at[span, center]),
+            (links + "top", SLOT[prefix + "T"] + i, array.at[span, top], ring.at[span, below]),
+            (links + "bot", SLOT[prefix + "B"] + i, array.at[span, bottom], ring.at[span, above]),
         )
 
     def raw_start(flows):
@@ -110,14 +133,27 @@
             start(*flow)
         home(*flows[0][1:], "start")
 
-    def raw_wait(flows):
-        for flow in flows:
+    def raw_center(flows):
+        arrive(*flows[0])
+        home(*flows[0][1:], "wait")
+
+    def raw_edges(flows):
+        for flow in flows[1:]:
             arrive(*flow)
-        home(*flows[0][1:], "wait")
-
-    flows_c = raw_flows("C", coef, ring_c, pl.ds(0, 3), lambda n: SLOT[n])
-    flows_l = [raw_flows("L", lam, ring_l, part(i), lambda n, i=i: SLOT[n] + i) for i in range(NC)]
-    flows_x = [raw_flows("X", dx, ring_x, part(i), lambda n, i=i: SLOT[n] + i) for i in range(NC)]
+
+    def on_flows(prefix, ring):
+        return [
+            (
+                ("on_top", SLOT[prefix + "F"] + i, ring.at[part(i), top], ring.at[part(i), below]),
+                ("on_bot", SLOT[prefix + "F"] + i, ring.at[part(i), bottom], ring.at[part(i), above]),
+            )
+            for i in range(NC)
+        ]
+
+    flows_c = raw_flows("C", coef, ring_c, pl.ds(0, 3), "araw_")
+    flows_l = [raw_flows("L", lam, ring_l, part(i), "own_", i) for i in range(NC)]
+    flows_x = [raw_flows("X", dx, ring_x, part(i), "own_", i) for i in range(NC)]
+    on_l, on_x = on_flows("L", ring_l), on_flows("X", ring_x)
 
     def halo_flows(prefix, ring):
         return [
@@ -141,36 +177,39 @@
     out_x = [("swap", SLOT["OX"] + i, ox_buf.at[part(i)], out_dx.at[part(i)]) for i in range(NC)]
     out_o = ("swap", SLOT["OO"], oo_buf, out_obs)
 
-    rings = (ring_l, ring_x, ring_p, ring_q, ring_c)
-
-    @pl.when(jnp.logical_not(not_first_t))
-    def _():
-        for ring in rings:
-            ring[:, rows + rows // 2:, :] = jnp.zeros((ring.shape[0], rows // 2, cols), F32)
-
-    @pl.when(jnp.logical_not(not_last_t))
-    def _():
-        for ring in rings:
-            ring[:, rows:rows + rows // 2, :] = jnp.zeros((ring.shape[0], rows // 2, cols), F32)
-
-    @pl.when(jnp.logical_not(not_last_k))
-    def _():
-        a_in[...] = jnp.zeros(a_in.shape, F32)
-        b_in[...] = jnp.zeros(b_in.shape, F32)
-
     aux[...] = jnp.zeros(aux.shape, F32)
+    for fetch in fetches:
+        fetch.wait()
     aux[0:1, :] = mult[...]
     aux[1:2, :] = fobs[...]
     aux[2:3, :] = ovar[...]
     aux[3:4, :] = oidx[...].astype(F32)
     aux[4:5, 0:levels] = sigma[...]
 
-    pl.semaphore_wait(barrier, sum(link[1].astype(jnp.int32) for link in links.values()))
+    pl.semaphore_wait(barrier, sum(peer[1].astype(jnp.int32) for peer in peers))
 
     raw_start(flows_c)
     start(*flow_aux)
     for i in range(NC):
         raw_start(flows_l[i])
+
+    rings = (ring_l, ring_x, ring_p, ring_q, ring_c)
+
+    @pl.when(jnp.logical_not(not_first_t))
+    def _():
+        for ring in rings:
+            ring[:, rows + rows // 2:, :] = jnp.zeros((ring.shape[0], rows // 2, cols), F32)
+
+    @pl.when(jnp.logical_not(not_last_t))
+    def _():
+        for ring in rings:
+            ring[:, rows:rows + rows // 2, :] = jnp.zeros((ring.shape[0], rows // 2, cols), F32)
+
+    @pl.when(jnp.logical_not(not_last_k))
+    def _():
+        a_in[...] = jnp.zeros(a_in.shape, F32)
+        b_in[...] = jnp.zeros(b_in.shape, F32)
+
     start(*fresh_0)
     start(*fresh_1)
 
@@ -238,13 +277,13 @@
 
     def vertical(ring, write):
         pad = jnp.zeros((deep - levels, cols), F32)
+        before, mid = ring[:, 2 * rows - 1, :], ring[:, 0, :]
         for y in range(rows):
-            def row(r):
-                return ring[:, (r + 2 * rows) % (2 * rows), :]
-            mid = row(y)
+            after = ring[:, y + 1, :]
             smooth = 0.6 * mid + 0.1 * (
-                row(y - 1) + row(y + 1) + pltpu.roll(mid, 1, 1) + pltpu.roll(mid, cols - 1, 1)
+                before + after + pltpu.roll(mid, 1, 1) + pltpu.roll(mid, cols - 1, 1)
             )
+            before, mid = mid, after
             high, low = halves(jnp.concatenate([smooth, pad], axis=0))
             stack = jnp.concatenate([high, low, high], axis=0)
             write(y, jnp.dot(v3[...], stack, preferred_element_type=F32))
@@ -252,14 +291,15 @@
     def store_dl(y, value):
         dl[:, y, :] = value
 
-    raw_wait(flows_c)
+    raw_center(flows_c)
+    raw_edges(flows_c)
     cen[...] = 1.0 - 2.0 * ring_c[0] - 2.0 * ring_c[1] - ring_c[2]
     rid = lax.broadcasted_iota(jnp.int32, (rows, cols), 0)
     inside = jnp.where(rid < rows // 2, not_last_t.astype(F32), not_first_t.astype(F32))
 
     def shifted(own, other, s):
-        wrap = rid < s if s > 0 else rid >= rows + s
-        return jnp.where(wrap, pltpu.roll(other, s % rows, 0), pltpu.roll(own, s % rows, 0))
+        wrap = rid >= rows - s if s > 0 else rid < -s
+        return pltpu.roll(jnp.where(wrap, other, own), s % rows, 0)
 
     def tl_tile(own, other, rs):
         near = shifted(own, other, 1) + shifted(own, other, -1)
@@ -301,16 +341,32 @@
             return carry
         lax.fori_loop(0, size // GROUP, some, 0)
 
-    for i in range(NC):
-        raw_wait(flows_l[i])
+    def do_l(i):
+        raw_center(flows_l[i])
+        for flow in on_l[i]:
+            start(*flow)
         raw_start(flows_x[i])
-
+        raw_edges(flows_l[i])
+        for flow in on_l[i]:
+            arrive(*flow)
+
+    def do_a(i):
         def body(l):
             a_buf[l] = ad_model(ring_l, l)
         for_levels(i, body)
         start(*down_a[i])
 
-    for i in range(NC):
+    def do_e(i):
+        raw_center(flows_x[i])
+        for flow in on_x[i]:
+            start(*flow)
+
+        def body(l):
+            e_buf[l] = dl[l] + ring_x[l, 0:rows, :]
+        for_levels(i, body)
+        start(*down_e[i])
+
+    def do_p(i):
         arrive(*down_a[i])
 
         def body(l):
@@ -318,76 +374,101 @@
         for_levels(i, body)
         for flow in halo_p[i]:
             start(*flow)
+
+    def do_m(i):
+        raw_edges(flows_x[i])
+        for flow in on_x[i]:
+            arrive(*flow)
+
+        def body(l):
+            m_buf[l] = jnp.where(not_last_k, tl_model(ring_x, l), 0.0)
+        for_levels(i, body)
+
+    def do_q(i):
+        arrive(*down_e[i])
+
+        def body(l):
+            ring_q[l, 0:rows, :] = e_in[l] - m_buf[l]
+        for_levels(i, body)
+        for flow in halo_q[i]:
+            start(*flow)
+
+    def do_n(i):
+        for flow in halo_p[i]:
+            arrive(*flow)
+
+        def body(l):
+            n_buf[l] = jnp.where(not_first_k, tl_model(ring_p, l), 0.0)
+        for_levels(i, body)
+
+    def do_b(i):
+        for flow in halo_q[i]:
+            arrive(*flow)
+
+        def body(l):
+            b_buf[l] = ad_model(ring_q, l)
+        for_levels(i, body)
+        start(*down_b[i])
+
+    def do_ol(i):
+        arrive(*down_p[i])
+
+        def body(l):
+            ol_buf[l] = dl[l] + (d2_in[l] - n_buf[l])
+        for_levels(i, body)
+        start(*out_l[i])
+        home(*out_l[i][1:], "start")
+
+    def do_ox(i):
+        arrive(*down_b[i])
+
+        def body(l):
+            ox_buf[l] = ring_q[l, 0:rows, :] - b_in[l] + ht[l]
+        for_levels(i, body)
+        start(*out_x[i])
+        home(*out_x[i][1:], "start")
+
+    for i in range(NC):
+        do_l(i)
+        do_a(i)
+    vertical(ring_l, store_dl)
+    do_p(0)
+    for i in range(NC):
+        do_e(i)
+        if i + 1 < NC:
+            do_p(i + 1)
+        do_m(i)
+        if i == 0:
+            arrive(*fresh_0)
+            arrive(*fresh_1)
+
+            @pl.when(fresh_own)
+            def _():
+                pltpu.make_async_copy(fresh.at[0], e_in, rsem.at[SLOT["F0"]]).wait()
+                pltpu.make_async_copy(fresh.at[1], d2_in, rsem.at[SLOT["F1"]]).wait()
+        else:
+            do_q(i - 1)
+    for i in range(NC):
         start(*down_p[i])
-
-    vertical(ring_l, store_dl)
-
-    for i in range(NC):
-        raw_wait(flows_x[i])
-
-        def body(l):
-            e_buf[l] = dl[l] + ring_x[l, 0:rows, :]
-        for_levels(i, body)
-        start(*down_e[i])
-
-        def body(l):
-            m_buf[l] = tl_model(ring_x, l)
-        for_levels(i, body)
-
     mu_buf[...] = jnp.broadcast_to(var * mu + sampled(ring_x[:, 0:rows, :]), mu_buf.shape)
     start(*down_mu)
-
-    arrive(*fresh_0)
-    arrive(*fresh_1)
-
-    @pl.when(fresh_own)
-    def _():
-        pltpu.make_async_copy(fresh.at[0], e_in, rsem.at[SLOT["F0"]]).wait()
-        pltpu.make_async_copy(fresh.at[1], d2_in, rsem.at[SLOT["F1"]]).wait()
+    do_q(NC - 1)
 
     @pl.when(jnp.logical_not(not_last_k))
     def _():
         mu_in[...] = jnp.broadcast_to(aux_in[1:2, :], mu_in.shape)
-        m_buf[...] = jnp.zeros(m_buf.shape, F32)
 
     for i in range(NC):
-        arrive(*down_e[i])
-
-        def body(l):
-            ring_q[l, 0:rows, :] = e_in[l] - m_buf[l]
-        for_levels(i, body)
-        for flow in halo_q[i]:
-            start(*flow)
-
-    keep_tl = not_first_k.astype(F32)
-    for i in range(NC):
-        for flow in halo_p[i]:
-            arrive(*flow)
-        arrive(*down_p[i])
-
-        def body(l):
-            n_buf[l] = d2_in[l] - keep_tl * tl_model(ring_p, l)
-        for_levels(i, body)
-
-    for i in range(NC):
-        for flow in halo_q[i]:
-            arrive(*flow)
-
-        def body(l):
-            b_buf[l] = ad_model(ring_q, l)
-        for_levels(i, body)
-        start(*down_b[i])
-
+        do_n(i)
+        if i == NC - 1:
+            arrive(*down_mu)
+            mu_two = mu_in[0:1, :]
+            spread(mu_two)
+        do_b(i)
+    do_ox(0)
     vertical(ring_q, store_dl)
     for i in range(NC):
-        def body(l):
-            ol_buf[l] = dl[l] + n_buf[l]
-        for_levels(i, body)
-        start(*out_l[i])
-        home(*out_l[i][1:], "start")
-
-    arrive(*down_mu)
-    mu_two = mu_in[0:1, :]
+        do_ol(i)
     oo_buf[...] = var * mu_two + sampled(d2_in[...])
     start(*out_o)
 
@@ -395,18 +476,11 @@
     def _():
         out_obs[...] = oo_buf[...]
 
-    spread(mu_two)
-    for i in range(NC):
-        arrive(*down_b[i])
-
-        def body(l):
-            ox_buf[l] = ring_q[l, 0:rows, :] - b_in[l] + ht[l]
-        for_levels(i, body)
-        start(*out_x[i])
-        home(*out_x[i][1:], "start")
+    for i in range(1, NC):
+        do_ox(i)
 
     everything = [flow_aux, fresh_0, fresh_1, down_mu, out_o, *flows_c]
-    for group in (*flows_l, *flows_x, *halo_p, *halo_q):
+    for group in (*flows_l, *flows_x, *on_l, *on_x, *halo_p, *halo_q):
         everything += list(group)
     everything += down_a + down_e + down_p + down_b + out_l + out_x
     for flow in everything:
@@ -415,6 +489,25 @@
         arrive(*flow)
         home(*flow[1:], "wait")
     arrive(*out_o)
+
+
+def hand_over(*refs):
+    sources, targets, stops, sems = refs[:3], refs[3:6], refs[6:9], refs[9]
+    inward, outward = [], []
+    for source, target, stop in zip(sources, targets, stops):
+        pieces = 3 if len(source.shape) == 3 else 1
+        step = source.shape[0] // pieces
+        for i in range(pieces):
+            span, n = pl.ds(i * step, step), len(inward)
+            inward.append(pltpu.make_async_copy(source.at[span], stop.at[span], sems.at[0, n]))
+            outward.append(pltpu.make_async_copy(stop.at[span], target.at[span], sems.at[1, n]))
+    for copy in inward:
+        copy.start()
+    for first, second in zip(inward, outward):
+        first.wait()
+        second.start()
+    for copy in outward:
+        copy.wait()
 
 
 def local(
@@ -444,7 +537,7 @@
             jax.ShapeDtypeStruct((1, nobs), F32),
             jax.ShapeDtypeStruct(field, F32),
         ),
-        in_specs=[anywhere, vmem, anywhere, anywhere, vmem, vmem, vmem, vmem, anywhere, vmem, vmem],
+        in_specs=[anywhere] * 11,
         out_specs=(anywhere, vmem, anywhere),
         scratch_shapes=[
             *[pltpu.VMEM(ring, F32)] * 4,
@@ -458,11 +551,19 @@
             pltpu.VMEM((1, nobs), F32),
             pltpu.VMEM((levels, 3 * deep), BF16),
             pltpu.VMEM((levels * rows, nobs), BF16),
+            pltpu.VMEM((1, nobs), F32),
+            pltpu.VMEM((1, nobs), F32),
+            pltpu.VMEM((1, levels), F32),
+            pltpu.VMEM((1, nobs), F32),
+            pltpu.VMEM((1, nobs), jnp.int32),
+            pltpu.VMEM(vert_cov.shape, F32),
+            pltpu.VMEM(block_pattern.shape, jnp.int32),
             pltpu.SemaphoreType.DMA((NSEM,)),
             pltpu.SemaphoreType.DMA((NSEM,)),
+            pltpu.SemaphoreType.DMA((7,)),
         ],
         compiler_params=pltpu.CompilerParams(
-            collective_id=0, has_side_effects=True, vmem_limit_bytes=48 * 2**20
+            collective_id=0, has_side_effects=True, vmem_limit_bytes=63 * 2**20
         ),
         cost_estimate=pl.CostEstimate(flops=10**9, bytes_accessed=5 * 10**6, transcendentals=0),
     )(
@@ -478,6 +579,19 @@
         vert_cov,
         block_pattern,
     )
+    results = (out_lam, out_obs, out_dx)
+    out_lam, out_obs, out_dx = pl.pallas_call(
+        hand_over,
+        name="hand_over",
+        out_shape=tuple(jax.ShapeDtypeStruct(r.shape, r.dtype) for r in results),
+        in_specs=[anywhere] * 3,
+        out_specs=(anywhere,) * 3,
+        scratch_shapes=[
+            *[pltpu.VMEM(r.shape, r.dtype) for r in results],
+            pltpu.SemaphoreType.DMA((2, 7)),
+        ],
+        compiler_params=pltpu.CompilerParams(vmem_limit_bytes=63 * 2**20),
+    )(*results)
     return out_lam[None], out_obs, out_dx[None]
 
 

time: 81.1 us -> 66.4 us (0.82)
  local copies, waits for them, and re-layouts: 11.2 us -> 0 us
  Pallas kernels: 68.8 us -> 65.5 us
    unnamed x25 -> x0, local copies, waits for them, and re-layouts: 11.2 us -> none
    pallas_call x1, Pallas kernels: 68.8 us -> 63.4 us  [local(): pl.pallas_call(kernel, name='saddle_slide', out_shape=(jax.ShapeDtypeStru...]
    pallas_call x0 -> x1, Pallas kernels: none -> 2.15 us  [local(): pl.pallas_call(hand_over, name='hand_over', out_shape=tuple((jax.ShapeDty...]
where the time goes in v2:
time: 66.4 us; the launch traced here: 66.1 us
  Pallas kernels  65.5 us (99%)
    pallas_call x1, Pallas kernels, local(): pl.pallas_call(kernel, name='saddle_slide', out_shape=(jax.ShapeDtypeStru...  63.4 us
    pallas_call x1, Pallas kernels, local(): pl.pallas_call(hand_over, name='hand_over', out_shape=tuple((jax.ShapeDty...  2.15 us

profile of v2, /device:TPU:1, one launch (start us, length us, event | category | flops | bytes accessed | tf_op | source)
XLA Modules:
  0.0 66.1 jit_solution(13937613893460454236)
XLA Ops:
  0.6 63.4 %saddle_slide.1 = (f32[72,8,256]{2,1,0:T(8,128)}, f32[1,256]{1,0:T(1,128)}, f32[72,8,256]{2,1,0:T(8,128)}) custom-call(f32[72,8,256]{2,1,0:T(8,128)} %bitcast.7, f32[1,256]{1,0:T(1,128)} %mult_hbm.1, f32[72,8,256]{2,1,0:T(8,128)} %bitcast.8, f32[2,72,8,256]{3,2,1,0:T(8,128)} %fresh.1, f32[1,256]{1,0:T(1,128)} %bitcast.11, f32[1,72]{1,0:T(1,128)} %sigma_hbm.1, ...), custom_call_target="tpu_custom_call" | custom-call | flops 1000000000 | bytes 5000000 | tf_op jit(solution)/shard_map/saddle_slide/pallas_call | solution.py:532
  64.0 2.2 %hand_over.1 = (f32[72,8,256]{2,1,0:T(8,128)}, f32[1,256]{1,0:T(1,128)}, f32[72,8,256]{2,1,0:T(8,128)}) custom-call(f32[72,8,256]{2,1,0:T(8,128)} %get-tuple-element.9.refs_0_, f32[1,256]{1,0:T(1,128)} %get-tuple-element.10.refs_1_, f32[72,8,256]{2,1,0:T(8,128)} %get-tuple-element.11.refs_2_), custom_call_target="tpu_custom_call" | custom-call | tf_op jit(solution)/shard_map/hand_over/pallas_call | solution.py:583

commit v3 on v2

--- a/solution.py
+++ b/solution.py
@@ -10,7 +10,7 @@
 BF16 = jnp.bfloat16
 LB = 8
 NC = 3
-GROUP = 4
+GROUP = 8
 CHUNKED = ("LC", "LT", "LB", "XC", "XT", "XB", "A", "E", "P", "B", "PT", "PB", "QT", "QB", "OL", "OX", "LF", "XF")
 SINGLE = ("CC", "CT", "CB", "AUX", "F0", "F1", "MU", "OO")
 SLOT = {name: i * NC for i, name in enumerate(CHUNKED)}
@@ -128,10 +128,17 @@
             (links + "bot", SLOT[prefix + "B"] + i, array.at[span, bottom], ring.at[span, above]),
         )
 
+    def start_center(flows):
+        start(*flows[0])
+        home(*flows[0][1:], "start")
+
+    def start_edges(flows):
+        for flow in flows[1:]:
+            start(*flow)
+
     def raw_start(flows):
-        for flow in flows:
-            start(*flow)
-        home(*flows[0][1:], "start")
+        start_center(flows)
+        start_edges(flows)
 
     def raw_center(flows):
         arrive(*flows[0])
@@ -345,7 +352,10 @@
         raw_center(flows_l[i])
         for flow in on_l[i]:
             start(*flow)
-        raw_start(flows_x[i])
+        start_center(flows_x[i])
+        if i == NC - 1:
+            for later in flows_x:
+                start_edges(later)
         raw_edges(flows_l[i])
         for flow in on_l[i]:
             arrive(*flow)
@@ -430,29 +440,30 @@
 
     for i in range(NC):
         do_l(i)
-        do_a(i)
+        if i < NC - 1:
+            do_a(i)
     vertical(ring_l, store_dl)
-    do_p(0)
     for i in range(NC):
         do_e(i)
-        if i + 1 < NC:
-            do_p(i + 1)
-        do_m(i)
-        if i == 0:
-            arrive(*fresh_0)
-            arrive(*fresh_1)
-
-            @pl.when(fresh_own)
-            def _():
-                pltpu.make_async_copy(fresh.at[0], e_in, rsem.at[SLOT["F0"]]).wait()
-                pltpu.make_async_copy(fresh.at[1], d2_in, rsem.at[SLOT["F1"]]).wait()
-        else:
-            do_q(i - 1)
+    do_a(NC - 1)
+    for i in range(NC):
+        if i > 0:
+            do_m(i - 1)
+        do_p(i)
+    do_m(NC - 1)
     for i in range(NC):
         start(*down_p[i])
+    arrive(*fresh_0)
+    arrive(*fresh_1)
+
+    @pl.when(fresh_own)
+    def _():
+        pltpu.make_async_copy(fresh.at[0], e_in, rsem.at[SLOT["F0"]]).wait()
+        pltpu.make_async_copy(fresh.at[1], d2_in, rsem.at[SLOT["F1"]]).wait()
+    for i in range(NC):
+        do_q(i)
     mu_buf[...] = jnp.broadcast_to(var * mu + sampled(ring_x[:, 0:rows, :]), mu_buf.shape)
     start(*down_mu)
-    do_q(NC - 1)
 
     @pl.when(jnp.logical_not(not_last_k))
     def _():

time: 66.4 us -> 64.5 us (0.971)
  Pallas kernels: 65.5 us -> 63.7 us
    pallas_call x1, Pallas kernels: 63.4 us -> 61.5 us  [local(): pl.pallas_call(kernel, name='saddle_slide', out_shape=(jax.ShapeDtypeStru...]
where the time goes in v3:
time: 64.5 us; the launch traced here: 64.3 us
  Pallas kernels  63.7 us (99%)
    pallas_call x1, Pallas kernels, local(): pl.pallas_call(kernel, name='saddle_slide', out_shape=(jax.ShapeDtypeStru...  61.5 us
    pallas_call x1, Pallas kernels, local(): pl.pallas_call(hand_over, name='hand_over', out_shape=tuple((jax.ShapeDty...  2.15 us

profile of v3, /device:TPU:1, one launch (start us, length us, event | category | flops | bytes accessed | tf_op | source)
XLA Modules:
  0.0 64.3 jit_solution(11027093052409158173)
XLA Ops:
  0.6 61.5 %saddle_slide.1 = (f32[72,8,256]{2,1,0:T(8,128)}, f32[1,256]{1,0:T(1,128)}, f32[72,8,256]{2,1,0:T(8,128)}) custom-call(f32[72,8,256]{2,1,0:T(8,128)} %bitcast.7, f32[1,256]{1,0:T(1,128)} %mult_hbm.1, f32[72,8,256]{2,1,0:T(8,128)} %bitcast.8, f32[2,72,8,256]{3,2,1,0:T(8,128)} %fresh.1, f32[1,256]{1,0:T(1,128)} %bitcast.11, f32[1,72]{1,0:T(1,128)} %sigma_hbm.1, ...), custom_call_target="tpu_custom_call" | custom-call | flops 1000000000 | bytes 5000000 | tf_op jit(solution)/shard_map/saddle_slide/pallas_call | solution.py:543
  62.2 2.2 %hand_over.1 = (f32[72,8,256]{2,1,0:T(8,128)}, f32[1,256]{1,0:T(1,128)}, f32[72,8,256]{2,1,0:T(8,128)}) custom-call(f32[72,8,256]{2,1,0:T(8,128)} %get-tuple-element.9.refs_0_, f32[1,256]{1,0:T(1,128)} %get-tuple-element.10.refs_1_, f32[72,8,256]{2,1,0:T(8,128)} %get-tuple-element.11.refs_2_), custom_call_target="tpu_custom_call" | custom-call | tf_op jit(solution)/shard_map/hand_over/pallas_call | solution.py:594
